TPU v7x, 256 devices: a whole 4x4x8 slice. The times are simulated.
256 devices in a mesh: leaf: 32 (over z, x), blk: 8 (over y, core).
Axes of the slice: x: 4, y: 4, z: 8, core: 2. Of those that a mesh axis runs over, the one named last changes fastest.
Arguments:
- rhs: float32 [6, 32, 4096], P(None, None, ('leaf', 'blk')), may hold values from -6 to 6
- diag_inverse: float32 [4096, 8064], P(('leaf', 'blk')), as said below
- off_diagonal: float32 [5, 4096, 512], P(None, ('leaf', 'blk')), may hold values from -0.1875 to 0.1875
- rows_index: int32 [5, 256, 512], P(None, ('leaf', 'blk')), may hold values from 0 to 7935, as said below
Outputs:
- solution: float32 [6, 32, 4096], P(None, None, ('leaf', 'blk'))
Inputs may be any that keep to these rules, and one draw needn't show every extreme that they name: `diag_inverse`: each level's packed block is lower triangular with a positive diagonal; entries to the right of a supernode's width within its level are zero. `rows_index`: an entry of level l lies below (2**6 - 2**(l+1)) * 128.
All inputs are finite; a program needn't handle non-finite values.
Results may differ from a plain program's by a relative error of at most 0.00013.
Values sent between devices are 32-bit elements; how exact they have to be, the bound alone decides.
No kernel may reach another device: no remote copies, remote signals or barrier semaphores. Data moves between devices by JAX's collectives and lax.ppermute only.
A program may use at most 64 MiB of HBM per device.

v0:
```python
import jax
import jax.numpy as jnp
from jax import lax
from jax.sharding import PartitionSpec as P


def from_partner(x, axis, apart):
    return lax.ppermute(x, axis, [(i, i ^ 1 << apart) for i in range(lax.axis_size(axis))])


def group_total(partial_value, height):
    summed = lax.psum(partial_value, "blk")
    for bit in range(height):
        summed = summed + from_partner(summed, "leaf", bit)
    return summed


def local(rhs, diag_inverse, off_diagonal, rows_index):
    highest = lax.Precision.HIGHEST
    levels_here = rhs.shape[0]
    species = rhs.shape[1]
    rows_block = rhs.shape[2]
    blk_count = lax.axis_size("blk")
    unit_rows = blk_count * rows_block
    chain_total = diag_inverse.shape[1]
    pos_leaf = lax.axis_index("leaf")
    pos_blk = lax.axis_index("blk")
    pending = jnp.zeros((species, chain_total), jnp.float32)
    for height in range(levels_here):
        offset = (2**height - 1) * unit_rows
        place = (jnp.remainder(pos_leaf, 2**height) * blk_count + pos_blk) * rows_block
        pending = lax.dynamic_update_slice(pending, rhs[height], (jnp.int32(0), offset + place))
    forward = []
    for height in range(levels_here):
        breadth = 2**height * unit_rows
        offset = (2**height - 1) * unit_rows
        current = group_total(pending[:, offset : offset + breadth], height)
        inverse_rows = diag_inverse[:, offset : offset + breadth]
        solved = lax.dot_general(
            current,
            inverse_rows,
            (((1,), (1,)), ((), ())),
            precision=highest,
            preferred_element_type=jnp.float32,
        )
        forward.append(solved)
        if height < levels_here - 1:
            update = jnp.dot(
                solved, off_diagonal[height], precision=highest, preferred_element_type=jnp.float32
            )
            targets = offset + breadth + rows_index[height, 0]
            pending = pending.at[:, targets].add(-update)
    known_chain = jnp.zeros((species, chain_total), jnp.float32)
    outputs = [None] * levels_here
    for height in reversed(range(levels_here)):
        breadth = 2**height * unit_rows
        offset = (2**height - 1) * unit_rows
        current = forward[height]
        if height < levels_here - 1:
            targets = offset + breadth + rows_index[height, 0]
            known = jnp.take(known_chain, targets, axis=1)
            coupling = lax.dot_general(
                known,
                off_diagonal[height],
                (((1,), (1,)), ((), ())),
                precision=highest,
                preferred_element_type=jnp.float32,
            )
            current = current - coupling
        inverse_rows = diag_inverse[:, offset : offset + breadth]
        partial_value = jnp.dot(
            current, inverse_rows, precision=highest, preferred_element_type=jnp.float32
        )
        solved = group_total(partial_value, height)
        known_chain = known_chain.at[:, offset : offset + breadth].set(solved)
        place = (jnp.remainder(pos_leaf, 2**height) * blk_count + pos_blk) * rows_block
        outputs[height] = lax.dynamic_slice_in_dim(solved, place, rows_block, 1)
    return jnp.stack(outputs, axis=0)


def solution(mesh):
    placed = (
        P(None, None, ("leaf", "blk")),
        P(("leaf", "blk"), None),
        P(None, ("leaf", "blk"), None),
        P(None, ("leaf", "blk"), None),
    )
    return jax.shard_map(
        local, mesh=mesh, in_specs=placed, out_specs=P(None, None, ("leaf", "blk")), check_vma=False
    )
```

profile of v0, /device:TPU:1, one launch (start us, length us, event | category | flops | bytes accessed | tf_op | source)
XLA Modules:
  0.0 1096.1 jit_solution(5668879297437034788)
XLA Ops:
  13.3 24.3 %psum.84 = f32[32,128]{0,1:T(8,128)S(1)} all-reduce(f32[32,128]{0,1:T(8,128)S(1)} %slice.231), channel_id=1, replica_groups=mesh['leaf'=32,'blk'=8] {'blk'}, use_global_device_ids=true, to_apply=%region_0.1 | all-reduce | flops 4096 | bytes 32768 | tf_op jit(solution)/shard_map/psum | solution.py:12
  38.1 7.1 scatter_fusion
  46.1 25.1 %psum.85 = f32[32,256]{0,1:T(8,128)S(1)} all-reduce(f32[32,256]{0,1:T(8,128)S(1)} %slice.232), channel_id=1, replica_groups=mesh['leaf'=32,'blk'=8] {'blk'}, use_global_device_ids=true, to_apply=%region_2.3 | all-reduce | flops 8192 | bytes 65536 | tf_op jit(solution)/shard_map/psum | solution.py:12
  75.7 7.1 scatter_fusion.1
  84.5 67.3 %all-reduce.10.cloned.1.call-done = f32[32,512]{0,1:T(8,128)} async-done(((f32[32,512]{0,1:T(8,128)}), f32[32,512]{0,1:T(8,128)}) %all-reduce.10.cloned.1.call-update) | async-done | bytes 65552 | tf_op jit(solution)/shard_map/psum | solution.py:12
  153.0 4.2 collective-permute-done.1
  161.0 4.4 collective-permute-done.2
  166.1 7.1 scatter_fusion.2
  175.1 71.0 %all-reduce.12.cloned.1.call-done = f32[32,1024]{0,1:T(8,128)} async-done(((f32[32,1024]{0,1:T(8,128)}), f32[32,1024]{0,1:T(8,128)}) %all-reduce.12.cloned.1.call-update) | async-done | bytes 131088 | tf_op jit(solution)/shard_map/psum | solution.py:12
  247.3 9.7 collective-permute-done.3
  261.0 8.6 collective-permute-done.4
  271.5 7.6 collective-permute-done.5
  279.9 7.1 scatter_fusion.3
  289.3 75.9 %all-reduce.14.cloned.1.call-done = f32[32,2048]{1,0:T(8,128)} async-done(((f32[32,2048]{1,0:T(8,128)}), f32[32,2048]{1,0:T(8,128)}) %all-reduce.14.cloned.1.call-update) | async-done | bytes 262160 | tf_op jit(solution)/shard_map/psum | solution.py:12
  366.4 4.2 collective-permute-done.6
  374.4 4.4 collective-permute-done.7
  380.2 3.9 collective-permute-done.8
  386.5 5.7 collective-permute-done.9
  393.0 7.1 scatter_fusion.4
  403.2 77.8 %all-reduce.16.cloned.1.call-done = f32[32,4096]{1,0:T(8,128)} async-done(((f32[32,4096]{1,0:T(8,128)}), f32[32,4096]{1,0:T(8,128)}) %all-reduce.16.cloned.1.call-update) | async-done | bytes 524304 | tf_op jit(solution)/shard_map/psum | solution.py:12
  482.2 9.7 collective-permute-done.10
  495.8 8.6 collective-permute-done.11
  505.9 7.6 collective-permute-done.12
  515.9 20.5 %collective-permute-done.13 = f32[32,4096]{1,0:T(8,128)S(1)} collective-permute-done((f32[32,4096]{1,0:T(8,128)S(1)}, f32[32,4096]{1,0:T(8,128)S(1)}, u32[]{:S(2)}, u32[]{:S(2)}) %collective-permute-start.13) | collective-permute-done | bytes 524320 | tf_op jit(solution)/shard_map/ppermute | solution.py:8
  536.4 7.1 collective-permute-start.14
  543.4 19.2 %collective-permute-done.14 = f32[32,4096]{1,0:T(8,128)S(1)} collective-permute-done((f32[32,4096]{1,0:T(8,128)S(1)}, f32[32,4096]{1,0:T(8,128)S(1)}, u32[]{:S(2)}, u32[]{:S(2)}) %collective-permute-start.14) | collective-permute-done | bytes 524320 | tf_op jit(solution)/shard_map/ppermute | solution.py:8
  564.7 78.3 %all-reduce.18.cloned.1.call-done = f32[32,4096]{1,0:T(8,128)} async-done(((f32[32,4096]{1,0:T(8,128)}), f32[32,4096]{1,0:T(8,128)}) %all-reduce.18.cloned.1.call-update) | async-done | bytes 524304 | tf_op jit(solution)/shard_map/psum | solution.py:12
  644.2 9.7 collective-permute-done.15
  658.0 8.6 collective-permute-done.16
  668.0 7.6 collective-permute-done.17
  678.0 20.4 %collective-permute-done.18 = f32[32,4096]{1,0:T(8,128)S(1)} collective-permute-done((f32[32,4096]{1,0:T(8,128)S(1)}, f32[32,4096]{1,0:T(8,128)S(1)}, u32[]{:S(2)}, u32[]{:S(2)}) %collective-permute-start.18) | collective-permute-done | bytes 524320 | tf_op jit(solution)/shard_map/ppermute | solution.py:8
  698.5 7.1 collective-permute-start.19
  705.6 19.2 %collective-permute-done.19 = f32[32,4096]{1,0:T(8,128)S(1)} collective-permute-done((f32[32,4096]{1,0:T(8,128)S(1)}, f32[32,4096]{1,0:T(8,128)S(1)}, u32[]{:S(2)}, u32[]{:S(2)}) %collective-permute-start.19) | collective-permute-done | bytes 524320 | tf_op jit(solution)/shard_map/ppermute | solution.py:8
  727.6 3.2 gather_fusion
  732.4 77.4 %all-reduce.20.cloned.1.call-done = f32[32,2048]{1,0:T(8,128)} async-done(((f32[32,2048]{1,0:T(8,128)}), f32[32,2048]{1,0:T(8,128)}) %all-reduce.20.cloned.1.call-update) | async-done | bytes 262160 | tf_op jit(solution)/shard_map/psum | solution.py:12
  811.0 4.2 collective-permute-done.20
  819.0 4.4 collective-permute-done.21
  824.8 3.9 collective-permute-done.22
  831.8 5.1 collective-permute-done.23
  840.3 3.2 gather_fusion.1
  844.9 76.3 %all-reduce.22.cloned.1.call-done = f32[32,1024]{1,0:T(8,128)} async-done(((f32[32,1024]{1,0:T(8,128)}), f32[32,1024]{1,0:T(8,128)}) %all-reduce.22.cloned.1.call-update) | async-done | bytes 131088 | tf_op jit(solution)/shard_map/psum | solution.py:12
  928.9 3.0 collective-permute-done.25
  939.6 3.2 gather_fusion.2
  944.2 66.7 %all-reduce.24.cloned.1.call-done = f32[32,512]{1,0:T(8,128)} async-done(((f32[32,512]{1,0:T(8,128)}), f32[32,512]{1,0:T(8,128)}) %all-reduce.24.cloned.1.call-update) | async-done | bytes 65552 | tf_op jit(solution)/shard_map/psum | solution.py:12
  1023.7 3.2 gather_fusion.3
  1027.5 24.8 %psum.94 = f32[32,256]{1,0:T(8,128)S(1)} all-reduce(f32[32,256]{1,0:T(8,128)S(1)} %fusion.70), channel_id=1, replica_groups=mesh['leaf'=32,'blk'=8] {'blk'}, use_global_device_ids=true, to_apply=%region_19.21 | all-reduce | flops 8192 | bytes 65536 | tf_op jit(solution)/shard_map/psum | solution.py:12
  1058.7 3.2 gather_fusion.4
  1062.5 25.2 %psum.95 = f32[32,128]{0,1:T(8,128)S(1)} all-reduce(f32[32,128]{0,1:T(8,128)S(1)} %fusion.73), channel_id=1, replica_groups=mesh['leaf'=32,'blk'=8] {'blk'}, use_global_device_ids=true, to_apply=%region_20.22 | all-reduce | flops 4096 | bytes 32768 | tf_op jit(solution)/shard_map/psum | solution.py:12
  (170 shorter events, 121.8 us)
Async XLA Ops:
  6.5 2.3 copy-start.2
  6.5 31.0 %copy-start = (f32[16,8064]{1,0:T(8,128)S(1)}, f32[16,8064]{1,0:T(8,128)}, u32[]{:S(2)}) copy-start(f32[16,8064]{1,0:T(8,128)} %param.17) | copy-start | bytes 1548292
  6.5 31.2 %copy-start.1 = (f32[5,16,512]{2,1,0:T(8,128)S(1)}, f32[5,16,512]{2,1,0:T(8,128)}, u32[]{:S(2)}) copy-start(f32[5,16,512]{2,1,0:T(8,128)} %param.18) | copy-start | bytes 491524
  6.5 31.6 %copy-start.3 = (s32[5,1,512]{2,1,0:T(1,128)S(1)}, s32[5,1,512]{2,1,0:T(1,128)}, u32[]{:S(2)}) copy-start(s32[5,1,512]{2,1,0:T(1,128)} %param.19) | copy-start | bytes 30724
  6.5 145.3 %all-reduce.10.cloned.1.call-start = ((), (), s32[]{:S(2)}) async-start(), calls=%async_computation | async-start | bytes 524288 | tf_op jit(solution)/shard_map/psum | solution.py:12
  71.2 3.9 collective-permute-start
  84.5 161.7 %all-reduce.12.cloned.1.call-start = ((), (), s32[]{:S(2)}) async-start(), calls=%async_computation.1 | async-start | bytes 1048576 | tf_op jit(solution)/shard_map/psum | solution.py:12
  151.8 5.4 collective-permute-start.1
  158.2 7.1 collective-permute-start.2
  175.1 190.1 %all-reduce.14.cloned.1.call-start = ((), (), s32[]{:S(2)}) async-start(), calls=%async_computation.2 | async-start | bytes 524288 | tf_op jit(solution)/shard_map/psum | solution.py:12
  246.1 10.9 collective-permute-start.3
  258.2 11.4 %collective-permute-start.4 = (f32[32,1024]{0,1:T(8,128)S(1)}, f32[32,1024]{0,1:T(8,128)S(1)}, u32[]{:S(2)}, u32[]{:S(2)}) collective-permute-start(f32[32,1024]{0,1:T(8,128)S(1)} %add.462), channel_id=1, source_target_pairs={{0,16},{8,24},{16,0},{24,8},{32,48},{40,56},{48,32},{56,40},{64,80... | collective-permute-start | bytes 393224 | tf_op jit(solution)/shard_map/ppermute | solution.py:8
  269.6 9.4 collective-permute-start.5
  289.3 191.7 %all-reduce.16.cloned.1.call-start = ((), (), s32[]{:S(2)}) async-start(), calls=%async_computation.3 | async-start | bytes 1048576 | tf_op jit(solution)/shard_map/psum | solution.py:12
  365.2 5.4 collective-permute-start.6
  371.6 7.1 collective-permute-start.7
  378.8 5.3 collective-permute-start.8
  384.1 8.1 collective-permute-start.9
  403.2 239.8 %all-reduce.18.cloned.1.call-start = ((), (), s32[]{:S(2)}) async-start(), calls=%async_computation.4 | async-start | bytes 1048576 | tf_op jit(solution)/shard_map/psum | solution.py:12
  481.0 10.9 collective-permute-start.10
  493.1 11.4 %collective-permute-start.11 = (f32[32,4096]{1,0:T(8,128)S(1)}, f32[32,4096]{1,0:T(8,128)S(1)}, u32[]{:S(2)}, u32[]{:S(2)}) collective-permute-start(f32[32,4096]{1,0:T(8,128)S(1)} %add.474), channel_id=1, source_target_pairs={{0,16},{8,24},{16,0},{24,8},{32,48},{40,56},{48,32},{56,40},{64,80... | collective-permute-start | bytes 1572872 | tf_op jit(solution)/shard_map/ppermute | solution.py:8
  504.5 9.0 collective-permute-start.12
  513.5 22.8 %collective-permute-start.13 = (f32[32,4096]{1,0:T(8,128)S(1)}, f32[32,4096]{1,0:T(8,128)S(1)}, u32[]{:S(2)}, u32[]{:S(2)}) collective-permute-start(f32[32,4096]{1,0:T(8,128)S(1)} %add.476), channel_id=1, source_target_pairs={{0,64},{8,72},{16,80},{24,88},{32,96},{40,104},{48,112},{56,120},{... | collective-permute-start | bytes 1572872 | tf_op jit(solution)/shard_map/ppermute | solution.py:8
  536.4 26.2 %collective-permute-start.14 = (f32[32,4096]{1,0:T(8,128)S(1)}, f32[32,4096]{1,0:T(8,128)S(1)}, u32[]{:S(2)}, u32[]{:S(2)}) collective-permute-start(f32[32,4096]{1,0:T(8,128)S(1)} %add.477), channel_id=1, source_target_pairs={{0,128},{8,136},{16,144},{24,152},{32,160},{40,168},{48,176},{56,1... | collective-permute-start | bytes 1572872 | tf_op jit(solution)/shard_map/ppermute | solution.py:8
  564.6 245.2 %all-reduce.20.cloned.1.call-start = ((), (), s32[]{:S(2)}) async-start(), calls=%async_computation.5 | async-start | bytes 524288 | tf_op jit(solution)/shard_map/psum | solution.py:12
  643.0 10.9 collective-permute-start.15
  655.0 11.6 %collective-permute-start.16 = (f32[32,4096]{1,0:T(8,128)S(1)}, f32[32,4096]{1,0:T(8,128)S(1)}, u32[]{:S(2)}, u32[]{:S(2)}) collective-permute-start(f32[32,4096]{1,0:T(8,128)S(1)} %add.479), channel_id=1, source_target_pairs={{0,16},{8,24},{16,0},{24,8},{32,48},{40,56},{48,32},{56,40},{64,80... | collective-permute-start | bytes 1572872 | tf_op jit(solution)/shard_map/ppermute | solution.py:8
  666.6 9.0 collective-permute-start.17
  675.7 22.8 %collective-permute-start.18 = (f32[32,4096]{1,0:T(8,128)S(1)}, f32[32,4096]{1,0:T(8,128)S(1)}, u32[]{:S(2)}, u32[]{:S(2)}) collective-permute-start(f32[32,4096]{1,0:T(8,128)S(1)} %add.481), channel_id=1, source_target_pairs={{0,64},{8,72},{16,80},{24,88},{32,96},{40,104},{48,112},{56,120},{... | collective-permute-start | bytes 1572872 | tf_op jit(solution)/shard_map/ppermute | solution.py:8
  698.5 26.2 %collective-permute-start.19 = (f32[32,4096]{1,0:T(8,128)S(1)}, f32[32,4096]{1,0:T(8,128)S(1)}, u32[]{:S(2)}, u32[]{:S(2)}) collective-permute-start(f32[32,4096]{1,0:T(8,128)S(1)} %add.482), channel_id=1, source_target_pairs={{0,128},{8,136},{16,144},{24,152},{32,160},{40,168},{48,176},{56,1... | collective-permute-start | bytes 1572872 | tf_op jit(solution)/shard_map/ppermute | solution.py:8
  732.3 188.8 %all-reduce.22.cloned.1.call-start = ((), (), s32[]{:S(2)}) async-start(), calls=%async_computation.6 | async-start | bytes 262144 | tf_op jit(solution)/shard_map/psum | solution.py:12
  809.8 5.4 collective-permute-start.20
  816.2 7.2 collective-permute-start.21
  823.4 5.3 collective-permute-start.22
  828.8 8.1 collective-permute-start.23
  844.8 166.1 %all-reduce.24.cloned.1.call-start = ((), (), s32[]{:S(2)}) async-start(), calls=%async_computation.7 | async-start | bytes 131072 | tf_op jit(solution)/shard_map/psum | solution.py:12
  921.2 4.0 collective-permute-start.24
  926.1 5.8 collective-permute-start.25
  932.0 4.2 collective-permute-start.26
  1010.9 3.3 collective-permute-start.27
  1015.1 5.2 collective-permute-start.28
  1052.3 3.1 collective-permute-start.29
  1087.8 0.6 copy-start.4
Sparse Core Ops, SparseCore 0:
  84.6 67.2 all-reduce.9
  175.2 70.9 all-reduce.11
  289.4 75.7 all-reduce.13
  403.3 77.6 all-reduce.15
  564.7 78.1 all-reduce.17
  732.5 77.2 all-reduce.19
  844.9 76.1 all-reduce.21
  944.2 66.6 all-reduce.23
where the time goes:
time: 1110 us; the launch traced here: 1100 us
  waiting for transfers between devices  808 us (73%)
  blocking collectives  99.3 us (9%)
  starting transfers between devices  67.2 us (6%)
  other arithmetic  49.3 us (4%)
  local copies, waits for them, and re-layouts  48.8 us (4%)
  between operations  14.2 us (1%)
    psum x8, waiting for transfers between devices, group_total(): summed = lax.psum(partial_value, 'blk')  591 us
    ppermute x30, waiting for transfers between devices, from_partner(): lax.ppermute(x, axis, [(i, i ^ 1 << apart) for i in range(lax.axis_size(a...  217 us
    psum x4, blocking collectives, group_total(): summed = lax.psum(partial_value, 'blk')  99.3 us
    ppermute x30, starting transfers between devices, from_partner(): lax.ppermute(x, axis, [(i, i ^ 1 << apart) for i in range(lax.axis_size(a...  66.8 us
    scatter-add x5, other arithmetic, local(): pending = pending.at[:, targets].add(-update)  35.3 us
  transfers between devices with their start and end apart: 38, of which 38 were waited for; matrix products, arithmetic and copies ran while one was open for 0% of the time, Pallas kernels for 0%

commit v1 on v0

v1 whole, which is shorter than its diff:
```python
import functools

import jax
import jax.numpy as jnp
from jax import lax
from jax.experimental import pallas as pl
from jax.experimental.pallas import tpu as pltpu
from jax.sharding import Mesh
from jax.sharding import PartitionSpec as P

PLANE = ("x", "blk")
LANES = 128
BLOCK = 16
BLOCKS = 32
ROWS = BLOCK * BLOCKS
REACH = 512
FIRST = (0, 8, 12, 16, 24, 40)
COUNT = (4, 4, 4, 8, 16, 32)
SPACE = 72
DIAG_AT = (0, 128, 384, 2688, 4224, 6784)
OFF_AT = (896, 1408, 1920, 3712, 6272)
AUX_AT = 2432
VMEM_LIMIT = 40 * 1024 * 1024


def pack_local(diag_inverse, off_diagonal, rows_index):
    named = rows_index[:, 0, :].astype(jnp.float32)
    aux = jnp.pad(named, ((0, 3), (0, 0))).reshape(BLOCK, 256)
    return jnp.concatenate(
        [
            diag_inverse[:, 0:896],
            off_diagonal[0],
            off_diagonal[1],
            off_diagonal[2],
            aux,
            diag_inverse[:, 896:1920],
            off_diagonal[3],
            diag_inverse[:, 1920:3968],
            off_diagonal[4],
            diag_inverse[:, 3968:8064],
        ],
        axis=1,
    )


def matvec(diag, at, groups, chunks, read_row, write):
    size = ROWS // groups
    for k in range(groups):
        for start in range(k * size, (k + 1) * size, 64):
            total = None
            for c in range(chunks):
                term = diag[start : start + 64, at + c * LANES : at + (c + 1) * LANES] * read_row(k * chunks + c)
                total = term if total is None else total + term
            write(start, jnp.sum(total, axis=1, keepdims=True))


def matvec_transposed(diag, at, groups, chunks, wide, write):
    size = ROWS // groups
    for k in range(groups):
        for c in range(chunks):
            total = None
            for start in range(k * size, (k + 1) * size, 64):
                term = diag[start : start + 64, at + c * LANES : at + (c + 1) * LANES] * wide[start : start + 64, :]
                total = term if total is None else total + term
            write(k * chunks + c, jnp.sum(total, axis=0, keepdims=True))


def scatter_update(off, at, wide, place, first, height):
    row_iota = lax.broadcasted_iota(jnp.int32, (height, REACH), 0) + first
    lane_iota = lax.broadcasted_iota(jnp.int32, (LANES, REACH), 0)

    def step(d, total):
        rows = off[pl.ds(pl.multiple_of(d * BLOCK, BLOCK), BLOCK), at : at + REACH]
        solved = wide[pl.ds(pl.multiple_of(d * BLOCK, BLOCK), BLOCK), :]
        solved = jnp.concatenate([solved] * (REACH // LANES), axis=1)
        update = jnp.sum(rows * solved, axis=0, keepdims=True)
        where = place[pl.ds(d, 1), :]
        high = jnp.right_shift(where, 7)
        low = jnp.bitwise_and(where, 127)
        coarse = update.astype(jnp.bfloat16).astype(jnp.float32)
        fine = update - coarse
        hit = row_iota == high
        left = jnp.concatenate(
            [
                jnp.where(hit, coarse, 0.0).astype(jnp.bfloat16),
                jnp.where(hit, fine, 0.0).astype(jnp.bfloat16),
            ],
            axis=0,
        )
        right = jnp.where(lane_iota == low, 1.0, 0.0).astype(jnp.bfloat16)
        return total + lax.dot_general(
            left, right, (((1,), (1,)), ((), ())), preferred_element_type=jnp.float32
        )

    total = lax.fori_loop(0, BLOCKS, step, jnp.zeros((2 * height, LANES), jnp.float32), unroll=4)
    return total[:height] + total[height:]


def gather_known(known, chain, place, first):
    tiles = [(i, j) for i in range(BLOCKS // 8) for j in range(REACH // LANES)]
    cut = [place[i * 8 : (i + 1) * 8, j * LANES : (j + 1) * LANES] for i, j in tiles]
    high = [jnp.right_shift(t, 7) for t in cut]
    low = [jnp.bitwise_and(t, 127) for t in cut]

    def step(h, values):
        row = jnp.broadcast_to(chain[pl.ds(h, 1), :], (8, LANES))
        return tuple(
            jnp.where(
                hi == h,
                jnp.take_along_axis(row, lo, axis=1, mode="promise_in_bounds"),
                v,
            )
            for hi, lo, v in zip(high, low, values)
        )

    zero = jnp.zeros((8, LANES), jnp.float32)
    values = lax.fori_loop(first, SPACE, step, tuple(zero for _ in tiles))
    for (i, j), v in zip(tiles, values):
        known[i * 8 : (i + 1) * 8, j * LANES : (j + 1) * LANES] = v


def couple(off, at, known, solved, column, wide):
    def step(d, carry):
        at_rows = pl.ds(pl.multiple_of(d * BLOCK, BLOCK), BLOCK)
        drop = jnp.sum(off[at_rows, at : at + REACH] * known[pl.ds(d, 1), :], axis=1, keepdims=True)
        wide[at_rows, :] = jnp.broadcast_to(solved[at_rows, column : column + 1] - drop, (BLOCK, LANES))
        return carry

    lax.fori_loop(0, BLOCKS, step, 0, unroll=4)


def forward_low(pack, start, solved, residual, places, held, wide, named, sems):
    copies = [
        pltpu.make_async_copy(pack.at[:, AUX_AT + k * LANES : AUX_AT + (k + 1) * LANES], named.at[k], sems.at[k + 1])
        for k in range(2)
    ]
    copies.append(pltpu.make_async_copy(pack.at[:, 0:AUX_AT], held, sems.at[0]))
    for copy in copies:
        copy.start()
    residual[...] = start[...]
    for copy in copies:
        copy.wait()
    block = lax.broadcasted_iota(jnp.int32, (BLOCKS, REACH), 0)
    for level in range(5):
        quarters = [
            named.at[a][pl.ds(2 * level + k, BLOCKS, stride=BLOCK), :] for k in range(2) for a in range(2)
        ]
        chain = jnp.concatenate(quarters, axis=1).astype(jnp.int32) + (2 ** (level + 1) - 1) * LANES
        shift = jnp.where((chain < 3 * LANES) & (block < 16), 8 * LANES - LANES, 9 * LANES)
        places[level] = chain + shift
    for level in range(3):
        groups = 4 >> level
        first = FIRST[level]

        def write(at, value, level=level):
            wide[at : at + 64, :] = jnp.broadcast_to(value, (64, LANES))
            solved[at : at + 64, level : level + 1] = value

        matvec(
            held, DIAG_AT[level], groups, 1 << level,
            lambda c, first=first: residual[first + c : first + c + 1, :], write,
        )
        update = scatter_update(held, OFF_AT[level], wide, places.at[level], 8, 64)
        residual[8:72, :] = residual[8:72, :] - update


def forward_high(level, pack, summed, before, places, solved, residual, held, wide, sems):
    first = FIRST[level + 1]
    columns = COUNT[level] * LANES
    copy = pltpu.make_async_copy(
        pack.at[:, DIAG_AT[level] : DIAG_AT[level] + columns + REACH], held, sems.at[0]
    )
    copy.start()
    residual[...] = before[...]
    copy.wait()

    def write(at, value):
        wide[at : at + 64, :] = jnp.broadcast_to(value, (64, LANES))
        solved[at : at + 64, 0:1] = value

    matvec(held, 0, 1, COUNT[level], lambda c: summed[c : c + 1, :], write)
    update = scatter_update(held, columns, wide, places.at[level], first, SPACE - first)
    residual[first:SPACE, :] = residual[first:SPACE, :] - update


def top(pack, summed, partial, held, wide, sems):
    copy = pltpu.make_async_copy(pack.at[:, DIAG_AT[5] : DIAG_AT[5] + 32 * LANES], held, sems.at[0])
    copy.start()
    copy.wait()

    def write(at, value):
        wide[at : at + 64, :] = jnp.broadcast_to(value, (64, LANES))

    matvec(held, 0, 1, COUNT[5], lambda c: summed[c : c + 1, :], write)

    def write_row(c, value):
        partial[c : c + 1, :] = value

    matvec_transposed(held, 0, 1, COUNT[5], wide, write_row)


def backward_high(level, pack, places, solved, *rest):
    above = rest[: 5 - level]
    partial, held, wide, chain, known, sems = rest[5 - level :]
    columns = COUNT[level] * LANES
    copy = pltpu.make_async_copy(
        pack.at[:, DIAG_AT[level] : DIAG_AT[level] + columns + REACH], held, sems.at[0]
    )
    copy.start()
    for k, value in enumerate(above):
        chain[FIRST[5 - k] : FIRST[5 - k] + COUNT[5 - k], :] = value[...]
    gather_known(known, chain, places.at[level], FIRST[level + 1])
    copy.wait()
    couple(held, columns, known, solved, 0, wide)

    def write_row(c, value):
        partial[c : c + 1, :] = value

    matvec_transposed(held, 0, 1, COUNT[level], wide, write_row)


def backward_low(pack, places, solved, s5, s4, s3, out, held, wide, chain, known, sems):
    copy = pltpu.make_async_copy(pack.at[:, 0:AUX_AT], held, sems.at[0])
    copy.start()
    for level, value in ((5, s5), (4, s4), (3, s3)):
        chain[FIRST[level] : FIRST[level] + COUNT[level], :] = value[...]
    chain[0:16, :] = jnp.zeros((16, LANES), jnp.float32)
    for level in (2, 1, 0):
        gather_known(known, chain, places.at[level], FIRST[level + 1])
        if level == 2:
            copy.wait()
        couple(held, OFF_AT[level], known, solved, level, wide)

        def write_row(c, value, first=FIRST[level]):
            chain[first + c : first + c + 1, :] = value

        matvec_transposed(held, DIAG_AT[level], 4 >> level, 1 << level, wide, write_row)
    out[...] = chain[0:16, :]


def call(body, outs, scratch, hbm_first, args):
    vmem = pl.BlockSpec(memory_space=pltpu.VMEM)
    specs = [pl.BlockSpec(memory_space=pl.ANY) if k == 0 and hbm_first else vmem for k in range(len(args))]
    return pl.pallas_call(
        body,
        out_shape=outs,
        in_specs=specs,
        out_specs=jax.tree.map(lambda _: vmem, outs),
        scratch_shapes=scratch + [pltpu.SemaphoreType.DMA((3,))],
        compiler_params=pltpu.CompilerParams(vmem_limit_bytes=VMEM_LIMIT),
    )(*args)


def shape(*dims, kind=jnp.float32):
    return jax.ShapeDtypeStruct(dims, kind)


def sum_planes(value, bits):
    for bit in range(bits):
        size = lax.axis_size("z")
        value = value + lax.ppermute(value, "z", [(i, i ^ 1 << bit) for i in range(size)])
    return value


def local(rhs, diag_inverse, off_diagonal, rows_index):
    f32 = jnp.float32
    plane = lax.axis_index("z")
    pack = lax.all_gather(pack_local(diag_inverse, off_diagonal, rows_index), PLANE, axis=0, tiled=True)
    mine = lax.all_to_all(jnp.transpose(rhs, (1, 0, 2)), PLANE, 0, 0)
    mine = jnp.transpose(mine, (1, 0, 2)).reshape(6, 4, LANES)
    start = jnp.zeros((SPACE, LANES), f32)
    for level in range(6):
        place = FIRST[level] + (jnp.remainder(plane, 2 ** (level - 2)) * 4 if level > 2 else 0)
        start = lax.dynamic_update_slice(start, mine[level], (place, 0))

    wide = pltpu.VMEM((ROWS, LANES), f32)
    solved_low, residual, places = call(
        forward_low,
        (shape(ROWS, 8), shape(SPACE, LANES), shape(5, BLOCKS, REACH, kind=jnp.int32)),
        [pltpu.VMEM((ROWS, AUX_AT), f32), wide, pltpu.VMEM((2, ROWS, LANES), f32)],
        True,
        (pack, start),
    )
    solved = {}
    for level in (3, 4):
        first, count = FIRST[level], COUNT[level]
        summed = sum_planes(residual[first : first + count], level - 2)
        solved[level], residual = call(
            functools.partial(forward_high, level),
            (shape(ROWS, 8), shape(SPACE, LANES)),
            [pltpu.VMEM((ROWS, count * LANES + REACH), f32), wide],
            True,
            (pack, summed, residual, places),
        )
    summed = sum_planes(residual[FIRST[5] : SPACE], 3)
    partial = call(
        top, shape(32, LANES), [pltpu.VMEM((ROWS, 32 * LANES), f32), wide], True, (pack, summed)
    )
    above = [sum_planes(partial, 3)]
    chain, known = pltpu.VMEM((SPACE, LANES), f32), pltpu.VMEM((BLOCKS, REACH), f32)
    for level in (4, 3):
        count = COUNT[level]
        partial = call(
            functools.partial(backward_high, level),
            shape(count, LANES),
            [pltpu.VMEM((ROWS, count * LANES + REACH), f32), wide, chain, known],
            True,
            (pack, places, solved[level], *above),
        )
        above.append(sum_planes(partial, level - 2))
    low = call(
        backward_low,
        shape(16, LANES),
        [pltpu.VMEM((ROWS, AUX_AT), f32), wide, chain, known],
        True,
        (pack, places, solved_low, *above),
    )
    pieces = [low[0:4], low[8:12], low[12:16]]
    for level in (3, 4, 5):
        place = jnp.remainder(plane, 2 ** (level - 2)) * 4
        pieces.append(lax.dynamic_slice_in_dim(above[5 - level], place, 4, 0))
    out = jnp.stack(pieces).reshape(6, BLOCKS, BLOCK)
    out = lax.all_to_all(jnp.transpose(out, (1, 0, 2)), PLANE, 0, 0)
    return jnp.transpose(out, (1, 0, 2))


def solution(mesh):
    split = Mesh(mesh.devices.reshape(8, 4, 8), ("z", "x", "blk"))
    rows = ("z", "x", "blk")
    placed = (P(None, None, rows), P(rows, None), P(None, rows, None), P(None, rows, None))
    return jax.shard_map(
        local, mesh=split, in_specs=placed, out_specs=P(None, None, rows), check_vma=False
    )
```

time: 1110 us -> 252 us (0.23); the launches traced: 1100 us -> 251 us
  waiting for transfers between devices: 808 us -> 98.5 us
  blocking collectives: 99.3 us -> 26.1 us
  Pallas kernels: 0 us -> 63.4 us
  other arithmetic: 49.3 us -> 0.75 us
  local copies, waits for them, and re-layouts: 48.8 us -> 11.9 us
  starting transfers between devices: 67.2 us -> 36.5 us
    psum x8 -> x0, waiting for transfers between devices: 591 us -> none  [group_total(): summed = lax.psum(partial_value, 'blk')]
    ppermute x30 -> x12, waiting for transfers between devices: 217 us -> 14.8 us  [sum_planes(): lax.ppermute(value, 'z', [(i, i ^ 1 << bit) for i in range(size)])]
    psum x4 -> x0, blocking collectives: 99.3 us -> none  [group_total(): summed = lax.psum(partial_value, 'blk')]
    all_gather x0 -> x1, waiting for transfers between devices: none -> 76 us  [local(): lax.all_gather(pack_local(diag_inverse, off_diagonal, rows_index), PLANE,...]
    pallas_call x0 -> x7, Pallas kernels: none -> 63.4 us  [call(): pl.pallas_call(body, out_shape=outs, in_specs=specs, out_specs=jax.tree.m...]
    ppermute x30 -> x12, starting transfers between devices: 66.8 us -> 27.9 us  [sum_planes(): lax.ppermute(value, 'z', [(i, i ^ 1 << bit) for i in range(size)])]
    scatter-add x5 -> x0, other arithmetic: 35.3 us -> none  [local(): pending = pending.at[:, targets].add(-update)]
    all_to_all x0 -> x1, blocking collectives: none -> 26.1 us  [local(): out = lax.all_to_all(jnp.transpose(out, (1, 0, 2)), PLANE, 0, 0)]
  transfers between devices with their start and end apart: 38 -> 14, of which waited for: 38 -> 14; matrix products, arithmetic and copies ran while one was open for 0% -> 1% of each run, Pallas kernels for 0% -> 0%
where the time goes in v1:
time: 252 us; the launch traced here: 251 us
  waiting for transfers between devices  98.5 us (39%)
  Pallas kernels  63.4 us (25%)
  starting transfers between devices  36.5 us (14%)
  blocking collectives  26.1 us (10%)
  between operations  13.7 us (5%)
  local copies, waits for them, and re-layouts  11.9 us (5%)
    all_gather x1, waiting for transfers between devices, local(): lax.all_gather(pack_local(diag_inverse, off_diagonal, rows_index), PLANE,...  76 us
    pallas_call x7, Pallas kernels, call(): pl.pallas_call(body, out_shape=outs, in_specs=specs, out_specs=jax.tree.m...  63.4 us
    ppermute x12, starting transfers between devices, sum_planes(): lax.ppermute(value, 'z', [(i, i ^ 1 << bit) for i in range(size)])  27.9 us
    all_to_all x1, blocking collectives, local(): out = lax.all_to_all(jnp.transpose(out, (1, 0, 2)), PLANE, 0, 0)  26.1 us
    ppermute x12, waiting for transfers between devices, sum_planes(): lax.ppermute(value, 'z', [(i, i ^ 1 << bit) for i in range(size)])  14.8 us
    unnamed x18, local copies, waits for them, and re-layouts  8.84 us
    all_to_all x1, starting transfers between devices, local(): mine = lax.all_to_all(jnp.transpose(rhs, (1, 0, 2)), PLANE, 0, 0)  8.59 us
    all_to_all x1, waiting for transfers between devices, local(): mine = lax.all_to_all(jnp.transpose(rhs, (1, 0, 2)), PLANE, 0, 0)  7.66 us
  transfers between devices with their start and end apart: 14, of which 14 were waited for; matrix products, arithmetic and copies ran while one was open for 1% of the time, Pallas kernels for 0%

profile of v1, /device:TPU:1, one launch (start us, length us, event | category | flops | bytes accessed | tf_op | source)
XLA Modules:
  0.0 250.8 jit_solution(12485761752629100055)
XLA Ops:
  6.5 0.7 convert_element_type.8
  7.3 0.8 slice_dynamic-update-slice_fusion.3
  8.1 0.8 constant_dynamic-update-slice_fusion.5
  8.9 0.8 constant_dynamic-update-slice_fusion.4
  9.6 0.8 constant_dynamic-update-slice_fusion.3
  10.4 0.8 slice_dynamic-update-slice_fusion.2
  11.2 0.8 constant_dynamic-update-slice_fusion.1
  12.0 0.9 slice_dynamic-update-slice_fusion.1
  12.9 0.8 constant_dynamic-update-slice_fusion
  13.7 1.0 slice_dynamic-update-slice_fusion
  14.7 0.9 copy-done
  15.5 1.6 copy.21
  17.1 8.6 %all-to-all-start = ((f32[32,6,16]{2,1,0:T(8,128)}), f32[32,6,16]{2,1,0:T(8,128)S(1)}, u32[]{:S(2)}, u32[]{:S(2)}) async-start(f32[32,6,16]{2,1,0:T(8,128)} %bitcast.5), calls=%async_computation | async-start | bytes 262144 | tf_op jit(solution)/shard_map/all_to_all | solution.py:269
  25.7 7.7 %all-to-all-done = f32[32,6,16]{2,1,0:T(8,128)S(1)} async-done(((f32[32,6,16]{2,1,0:T(8,128)}), f32[32,6,16]{2,1,0:T(8,128)S(1)}, u32[]{:S(2)}, u32[]{:S(2)}) %all-to-all-start) | async-done | bytes 12320 | tf_op jit(solution)/shard_map/all_to_all | solution.py:269
  34.3 76.0 %all-gather.2.cloned.1.call-done.pack = f32[512,10880]{1,0:T(8,128)} async-done(((f32[16,10880]{1,0:T(8,128)}), f32[512,10880]{1,0:T(8,128)}) %all-gather.2.cloned.1.call-update) | async-done | bytes 22282256 | tf_op jit(solution)/shard_map/all_gather | solution.py:268
  110.3 10.8 %shard_map.46 = (f32[512,8]{1,0:T(8,128)S(1)}, f32[72,128]{1,0:T(8,128)S(1)}, s32[5,32,512]{2,1,0:T(8,128)S(1)}) custom-call(f32[512,10880]{1,0:T(8,128)} %all-gather.2.cloned.1.call-done.pack, f32[72,128]{1,0:T(8,128)S(1)} %constant_dynamic-update-slice_fusion.12.start), custom_call_target="tpu_custom_call" | custom-call | tf_op jit(solution)/shard_map/pallas_call | solution.py:244
  121.1 1.4 collective-permute-start
  122.5 1.2 collective-permute-done
  123.7 4.6 %shard_map.47 = (f32[512,8]{1,0:T(8,128)S(1)}, f32[72,128]{1,0:T(8,128)S(1)}) custom-call(f32[512,10880]{1,0:T(8,128)} %all-gather.2.cloned.1.call-done.pack, f32[8,128]{1,0:T(8,128)S(1)} %slice_add_fusion.summed, f32[72,128]{1,0:T(8,128)S(1)} %get-tuple-element.14.before, s32[5,32,512]{2,1,0:T(8,128)S(1)} %get-tuple-element.12.places), custom_call_target="tpu_custom_call" | custom-call | tf_op jit(solution)/shard_map/pallas_call | solution.py:244
  128.3 1.4 collective-permute-start.1
  129.7 1.2 collective-permute-done.1
  130.9 2.3 collective-permute-start.2
  133.2 1.1 collective-permute-done.2
  134.3 5.4 %shard_map.48 = (f32[512,8]{1,0:T(8,128)S(1)}, f32[72,128]{1,0:T(8,128)S(1)}) custom-call(f32[512,10880]{1,0:T(8,128)} %all-gather.2.cloned.1.call-done.pack, f32[16,128]{1,0:T(8,128)S(1)} %add.89.summed, f32[72,128]{1,0:T(8,128)S(1)} %get-tuple-element.15.before, s32[5,32,512]{2,1,0:T(8,128)S(1)} %get-tuple-element.12.places), custom_call_target="tpu_custom_call" | custom-call | tf_op jit(solution)/shard_map/pallas_call | solution.py:244
  139.7 1.4 collective-permute-start.3
  141.1 1.3 collective-permute-done.3
  142.4 2.3 collective-permute-start.4
  144.6 1.2 collective-permute-done.4
  145.9 5.5 %collective-permute-start.5 = (f32[32,128]{1,0:T(8,128)S(1)}, f32[32,128]{1,0:T(8,128)S(1)}, u32[]{:S(2)}, u32[]{:S(2)}) collective-permute-start(f32[32,128]{1,0:T(8,128)S(1)} %add.91), channel_id=1, source_target_pairs={{0,128},{32,160},{64,192},{96,224},{128,0},{160,32},{192,64},{224,... | collective-permute-start | bytes 49160 | tf_op jit(solution)/shard_map/ppermute | solution.py:261
  151.3 1.1 collective-permute-done.5
  152.5 5.3 %shard_map.49 = f32[32,128]{1,0:T(8,128)S(1)} custom-call(f32[512,10880]{1,0:T(8,128)} %all-gather.2.cloned.1.call-done.pack, f32[32,128]{1,0:T(8,128)S(1)} %add.92.summed), custom_call_target="tpu_custom_call" | custom-call | tf_op jit(solution)/shard_map/pallas_call | solution.py:244
  157.7 1.3 collective-permute-start.6
  159.0 1.4 collective-permute-done.6
  160.4 2.3 collective-permute-start.7
  162.7 1.2 collective-permute-done.7
  163.9 5.4 %collective-permute-start.8 = (f32[32,128]{1,0:T(8,128)S(1)}, f32[32,128]{1,0:T(8,128)S(1)}, u32[]{:S(2)}, u32[]{:S(2)}) collective-permute-start(f32[32,128]{1,0:T(8,128)S(1)} %add.94), channel_id=1, source_target_pairs={{0,128},{32,160},{64,192},{96,224},{128,0},{160,32},{192,64},{224,... | collective-permute-start | bytes 49160 | tf_op jit(solution)/shard_map/ppermute | solution.py:261
  169.4 1.1 collective-permute-done.8
  170.5 5.6 %shard_map.50 = f32[16,128]{1,0:T(8,128)S(1)} custom-call(f32[512,10880]{1,0:T(8,128)} %all-gather.2.cloned.1.call-done.pack, s32[5,32,512]{2,1,0:T(8,128)S(1)} %get-tuple-element.12.places, f32[512,8]{1,0:T(8,128)S(1)} %get-tuple-element.17.solved, f32[32,128]{1,0:T(8,128)S(1)} %add.95.rest_0_.s5), custom_call_target="tpu_custom_call" | custom-call | tf_op jit(solution)/shard_map/pallas_call | solution.py:244
  176.1 1.2 collective-permute-start.9
  177.3 1.7 collective-permute-done.9
  179.0 2.3 collective-permute-start.10
  181.4 1.0 collective-permute-done.10
  182.4 7.1 %shard_map.51 = f32[8,128]{1,0:T(8,128)S(1)} custom-call(f32[512,10880]{1,0:T(8,128)} %all-gather.2.cloned.1.call-done.pack, s32[5,32,512]{2,1,0:T(8,128)S(1)} %get-tuple-element.12.places, f32[512,8]{1,0:T(8,128)S(1)} %get-tuple-element.18.solved, f32[32,128]{1,0:T(8,128)S(1)} %add.95.rest_0_.s5, f32[16,128]{1,0:T(8,128)S(1)} %add.97.rest_1_.s4), custom_call_target="tpu_custom_call" | custom-call | tf_op jit(solution)/shard_map/pallas_call | solution.py:244
  189.5 1.3 collective-permute-start.11
  191.0 1.1 collective-permute-done.11
  192.1 24.6 %shard_map.52 = f32[16,128]{1,0:T(8,128)S(1)} custom-call(f32[512,10880]{1,0:T(8,128)} %all-gather.2.cloned.1.call-done.pack, s32[5,32,512]{2,1,0:T(8,128)S(1)} %get-tuple-element.12.places, f32[512,8]{1,0:T(8,128)S(1)} %get-tuple-element.13.solved, f32[32,128]{1,0:T(8,128)S(1)} %add.95.rest_0_.s5, f32[16,128]{1,0:T(8,128)S(1)} %add.97.rest_1_.s4, ...), custom_call_target="tpu_custom_call" | custom-call | tf_op jit(solution)/shard_map/pallas_call | solution.py:244
  217.1 26.1 %all_to_all.10 = f32[32,6,16]{2,1,0:T(8,128)S(1)} all-to-all(f32[32,6,16]{2,1,0:T(8,128)S(1)} %copy.22), channel_id=1, replica_groups=mesh['z'=8,'x'=4,'blk'=8] {'x','blk'}, dimensions={0} | all-to-all | bytes 24576 | tf_op jit(solution)/shard_map/all_to_all | solution.py:323
  243.3 0.7 copy.23
  (52 shorter events, 1.5 us)
Async XLA Ops:
  6.5 103.7 %all-gather.2.cloned.1.call-start = ((), (), s32[]{:S(2)}) async-start(), calls=%async_computation.2 | async-start | bytes 22978560 | tf_op jit(solution)/shard_map/all_gather | solution.py:268
  14.6 0.9 copy-start
  17.1 16.3 %all-to-all-start = ((f32[32,6,16]{2,1,0:T(8,128)}), f32[32,6,16]{2,1,0:T(8,128)S(1)}, u32[]{:S(2)}, u32[]{:S(2)}) async-start(f32[32,6,16]{2,1,0:T(8,128)} %bitcast.5), calls=%async_computation | async-start | bytes 262144 | tf_op jit(solution)/shard_map/all_to_all | solution.py:269
  121.1 2.5 %collective-permute-start = (f32[8,128]{1,0:T(8,128)S(1)}, f32[8,128]{1,0:T(8,128)S(1)}, u32[]{:S(2)}, u32[]{:S(2)}) collective-permute-start(f32[8,128]{1,0:T(8,128)S(1)} %slice.84), channel_id=1, source_target_pairs={{0,32},{32,0},{64,96},{96,64},{128,160},{160,128},{192,224},{224,1... | collective-permute-start | bytes 12296 | tf_op jit(solution)/shard_map/ppermute | solution.py:261
  128.3 2.6 %collective-permute-start.1 = (f32[16,128]{1,0:T(8,128)S(1)}, f32[16,128]{1,0:T(8,128)S(1)}, u32[]{:S(2)}, u32[]{:S(2)}) collective-permute-start(f32[16,128]{1,0:T(8,128)S(1)} %slice.85), channel_id=1, source_target_pairs={{0,32},{32,0},{64,96},{96,64},{128,160},{160,128},{192,224},{224,1... | collective-permute-start | bytes 24584 | tf_op jit(solution)/shard_map/ppermute | solution.py:261
  130.9 3.4 %collective-permute-start.2 = (f32[16,128]{1,0:T(8,128)S(1)}, f32[16,128]{1,0:T(8,128)S(1)}, u32[]{:S(2)}, u32[]{:S(2)}) collective-permute-start(f32[16,128]{1,0:T(8,128)S(1)} %slice_add_fusion.1), channel_id=1, source_target_pairs={{0,64},{32,96},{64,0},{96,32},{128,192},{160,224},{192,128},{224,1... | collective-permute-start | bytes 24584 | tf_op jit(solution)/shard_map/ppermute | solution.py:261
  139.7 2.7 %collective-permute-start.3 = (f32[32,128]{1,0:T(8,128)S(1)}, f32[32,128]{1,0:T(8,128)S(1)}, u32[]{:S(2)}, u32[]{:S(2)}) collective-permute-start(f32[32,128]{1,0:T(8,128)S(1)} %slice.86), channel_id=1, source_target_pairs={{0,32},{32,0},{64,96},{96,64},{128,160},{160,128},{192,224},{224,1... | collective-permute-start | bytes 49160 | tf_op jit(solution)/shard_map/ppermute | solution.py:261
  142.4 3.5 %collective-permute-start.4 = (f32[32,128]{1,0:T(8,128)S(1)}, f32[32,128]{1,0:T(8,128)S(1)}, u32[]{:S(2)}, u32[]{:S(2)}) collective-permute-start(f32[32,128]{1,0:T(8,128)S(1)} %slice_add_fusion.2), channel_id=1, source_target_pairs={{0,64},{32,96},{64,0},{96,32},{128,192},{160,224},{192,128},{224,1... | collective-permute-start | bytes 49160 | tf_op jit(solution)/shard_map/ppermute | solution.py:261
  145.9 6.6 %collective-permute-start.5 = (f32[32,128]{1,0:T(8,128)S(1)}, f32[32,128]{1,0:T(8,128)S(1)}, u32[]{:S(2)}, u32[]{:S(2)}) collective-permute-start(f32[32,128]{1,0:T(8,128)S(1)} %add.91), channel_id=1, source_target_pairs={{0,128},{32,160},{64,192},{96,224},{128,0},{160,32},{192,64},{224,... | collective-permute-start | bytes 49160 | tf_op jit(solution)/shard_map/ppermute | solution.py:261
  157.7 2.7 %collective-permute-start.6 = (f32[32,128]{1,0:T(8,128)S(1)}, f32[32,128]{1,0:T(8,128)S(1)}, u32[]{:S(2)}, u32[]{:S(2)}) collective-permute-start(f32[32,128]{1,0:T(8,128)S(1)} %shard_map.49), channel_id=1, source_target_pairs={{0,32},{32,0},{64,96},{96,64},{128,160},{160,128},{192,224},{224,1... | collective-permute-start | bytes 49160 | tf_op jit(solution)/shard_map/ppermute | solution.py:261
  160.4 3.5 %collective-permute-start.7 = (f32[32,128]{1,0:T(8,128)S(1)}, f32[32,128]{1,0:T(8,128)S(1)}, u32[]{:S(2)}, u32[]{:S(2)}) collective-permute-start(f32[32,128]{1,0:T(8,128)S(1)} %add.93), channel_id=1, source_target_pairs={{0,64},{32,96},{64,0},{96,32},{128,192},{160,224},{192,128},{224,1... | collective-permute-start | bytes 49160 | tf_op jit(solution)/shard_map/ppermute | solution.py:261
  163.9 6.6 %collective-permute-start.8 = (f32[32,128]{1,0:T(8,128)S(1)}, f32[32,128]{1,0:T(8,128)S(1)}, u32[]{:S(2)}, u32[]{:S(2)}) collective-permute-start(f32[32,128]{1,0:T(8,128)S(1)} %add.94), channel_id=1, source_target_pairs={{0,128},{32,160},{64,192},{96,224},{128,0},{160,32},{192,64},{224,... | collective-permute-start | bytes 49160 | tf_op jit(solution)/shard_map/ppermute | solution.py:261
  176.1 2.9 %collective-permute-start.9 = (f32[16,128]{1,0:T(8,128)S(1)}, f32[16,128]{1,0:T(8,128)S(1)}, u32[]{:S(2)}, u32[]{:S(2)}) collective-permute-start(f32[16,128]{1,0:T(8,128)S(1)} %shard_map.50), channel_id=1, source_target_pairs={{0,32},{32,0},{64,96},{96,64},{128,160},{160,128},{192,224},{224,1... | collective-permute-start | bytes 24584 | tf_op jit(solution)/shard_map/ppermute | solution.py:261
  179.0 3.4 %collective-permute-start.10 = (f32[16,128]{1,0:T(8,128)S(1)}, f32[16,128]{1,0:T(8,128)S(1)}, u32[]{:S(2)}, u32[]{:S(2)}) collective-permute-start(f32[16,128]{1,0:T(8,128)S(1)} %add.96), channel_id=1, source_target_pairs={{0,64},{32,96},{64,0},{96,32},{128,192},{160,224},{192,128},{224,1... | collective-permute-start | bytes 24584 | tf_op jit(solution)/shard_map/ppermute | solution.py:261
  189.5 2.5 %collective-permute-start.11 = (f32[8,128]{1,0:T(8,128)S(1)}, f32[8,128]{1,0:T(8,128)S(1)}, u32[]{:S(2)}, u32[]{:S(2)}) collective-permute-start(f32[8,128]{1,0:T(8,128)S(1)} %shard_map.51), channel_id=1, source_target_pairs={{0,32},{32,0},{64,96},{96,64},{128,160},{160,128},{192,224},{224,1... | collective-permute-start | bytes 12296 | tf_op jit(solution)/shard_map/ppermute | solution.py:261
Sparse Core Ops, SparseCore 0:
  15.7 94.5 all-gather.1

commit v2 on v0

v2 whole, which is shorter than its diff:
```python
import functools

import jax
import jax.numpy as jnp
from jax import lax
from jax.experimental import pallas as pl
from jax.experimental.pallas import tpu as pltpu
from jax.sharding import Mesh
from jax.sharding import PartitionSpec as P

PLANE = ("x", "blk")
LANES = 128
BLOCK = 16
BLOCKS = 32
ROWS = BLOCK * BLOCKS
REACH = 512
SLOTS = 8
OWN = SLOTS * BLOCK
SPECIES = 4
FIRST = (0, 8, 12, 16, 24, 40)
COUNT = (4, 4, 4, 8, 16, 32)
SPACE = 72
PATH = 64
PARTS = 10
DIAG_AT = (512, 1152, 1920, 2944, 0, 2048)
OFF_AT = (640, 1408, 2432, 3968, 6144)
NAMED_AT = (0, 6656)
RHS_AT = 256
CUT = 1920
LOW = 4480
HIGH = 6912
LEVEL_AT = ((0, 1152), (1152, 1920), (1920, 2944), (2944, 4480))
MIB = 1024 * 1024


def pack_kernel(rhs, rows_index, diag_inverse, off_diagonal, high, low, first, second, sems):
    moves = [(diag_inverse.at[:, 1920:8064], high.at[:, 0:6144])]
    moves.append((off_diagonal.at[4], high.at[:, OFF_AT[4] : OFF_AT[4] + REACH]))
    for level in range(4):
        part, at = (first, 0) if level < 2 else (second, CUT)
        columns = 2**level * LANES
        diag = diag_inverse.at[:, columns - LANES : 2 * columns - LANES]
        for to, less in ((part, at), (low, 0)):
            first_at, second_at = DIAG_AT[level] - less, OFF_AT[level] - less
            moves.append((diag, to.at[:, first_at : first_at + columns]))
            moves.append((off_diagonal.at[level], to.at[:, second_at : second_at + REACH]))
    copies = [pltpu.make_async_copy(source, target, sems.at[k]) for k, (source, target) in enumerate(moves)]
    for copy in copies:
        copy.start()
    given = jnp.concatenate(
        [jnp.transpose(rhs[...].reshape(192, BLOCK)), jnp.zeros((BLOCK, 64), jnp.float32)], axis=1
    )
    for to in (first, low):
        to[:, RHS_AT : RHS_AT + 256] = given
    for to, at in ((first, NAMED_AT[0]), (low, NAMED_AT[0]), (high, NAMED_AT[1])):
        for level in range(5):
            for k in range(2):
                named = rows_index[level, :, k * 256 : (k + 1) * 256].astype(jnp.float32)
                to[2 * level + k : 2 * level + k + 1, at : at + 256] = named
        to[10:16, at : at + 256] = jnp.zeros((6, 256), jnp.float32)
    for copy in copies:
        copy.wait()


def matvec(diag, at, groups, chunks, read_row, write, rows=ROWS):
    size = rows // groups
    for k in range(groups):
        for start in range(k * size, (k + 1) * size, 64):
            total = None
            for c in range(chunks):
                term = diag[start : start + 64, at + c * LANES : at + (c + 1) * LANES] * read_row(k * chunks + c)
                total = term if total is None else total + term
            write(start, jnp.sum(total, axis=1, keepdims=True))


def matvec_transposed(diag, at, groups, chunks, wide, write, rows=ROWS):
    size = rows // groups
    for k in range(groups):
        for c in range(chunks):
            total = None
            for start in range(k * size, (k + 1) * size, 64):
                term = diag[start : start + 64, at + c * LANES : at + (c + 1) * LANES] * wide[start : start + 64, :]
                total = term if total is None else total + term
            write(k * chunks + c, jnp.sum(total, axis=0, keepdims=True))


def split(value):
    coarse = value.astype(jnp.bfloat16)
    return coarse, (value - coarse.astype(jnp.float32)).astype(jnp.bfloat16)


def one_hot(where, rows, first):
    names = lax.broadcasted_iota(jnp.int32, (rows, REACH), 0) + first
    return names == where


def block_rows(d):
    return pl.ds(pl.multiple_of(d * BLOCK, BLOCK), BLOCK)


def scatter_update(off, at, wide, place, first, height):
    def step(d, total):
        solved = wide[block_rows(d), :]
        solved = jnp.concatenate([solved] * (REACH // LANES), axis=1)
        update = jnp.sum(off[block_rows(d), at : at + REACH] * solved, axis=0, keepdims=True)
        where = place[pl.ds(d, 1), :]
        hit = one_hot(jnp.right_shift(where, 7), height, first)
        coarse = update.astype(jnp.bfloat16).astype(jnp.float32)
        left = jnp.concatenate(
            [jnp.where(hit, part, 0.0).astype(jnp.bfloat16) for part in (coarse, update - coarse)], axis=0
        )
        right = one_hot(jnp.bitwise_and(where, 127), LANES, 0).astype(jnp.bfloat16)
        return total + lax.dot_general(
            left, right, (((1,), (1,)), ((), ())), preferred_element_type=jnp.float32
        )

    total = lax.fori_loop(0, BLOCKS, step, jnp.zeros((2 * height, LANES), jnp.float32), unroll=4)
    return total[:height] + total[height:]


def couple(off, at, chain, place, first, solved, column, wide):
    height = SPACE - first
    table = jnp.concatenate(split(chain[first:SPACE, :]), axis=0)

    def step(d, carry):
        where = place[pl.ds(d, 1), :]
        right = one_hot(jnp.bitwise_and(where, 127), LANES, 0).astype(jnp.bfloat16)
        rows = jnp.dot(table, right, preferred_element_type=jnp.float32)
        hit = one_hot(jnp.right_shift(where, 7), height, first)
        known = jnp.sum(jnp.where(hit, rows[:height] + rows[height:], 0.0), axis=0, keepdims=True)
        drop = jnp.sum(off[block_rows(d), at : at + REACH] * known, axis=1, keepdims=True)
        wide[block_rows(d), :] = jnp.broadcast_to(
            solved[block_rows(d), column : column + 1] - drop, (BLOCK, LANES)
        )
        return carry

    lax.fori_loop(0, BLOCKS, step, 0, unroll=4)


def fetch(pack, held, sems, cuts):
    copies = []
    for k, (first, last, to) in enumerate(cuts):
        copies.append(
            pltpu.make_async_copy(pack.at[:, first:last], held.at[:, to : to + last - first], sems.at[k])
        )
        copies[-1].start()
    return copies


def fetch_named(pack, named, sems, at, which):
    first = NAMED_AT[which]
    copies = [
        pltpu.make_async_copy(pack.at[:, first + k * LANES : first + (k + 1) * LANES], named.at[k], sems.at[at + k])
        for k in range(2)
    ]
    for copy in copies:
        copy.start()
    return copies


def chain_position(named, level, blocks):
    quarters = [
        named.at[a][pl.ds(2 * level + k, blocks, stride=BLOCK), :] for k in range(2) for a in range(2)
    ]
    return jnp.concatenate(quarters, axis=1).astype(jnp.int32) + (2 ** (level + 1) - 1) * LANES


def find_places(named, level, places):
    chain = chain_position(named, level, BLOCKS)
    if level == 0:
        block = lax.broadcasted_iota(jnp.int32, (BLOCKS, REACH), 0)
        places[...] = chain + jnp.where((chain < 3 * LANES) & (block < 16), 7 * LANES, 9 * LANES)
    else:
        places[...] = chain + 9 * LANES


def fetch_parts(parts, level, held, sems):
    first, last = LEVEL_AT[level]
    less = 0 if level < 2 else CUT
    copies, at = [], 0
    for k, part in enumerate(parts):
        count = part.shape[0]
        copies.append(
            pltpu.make_async_copy(part.at[:, first - less : last - less], held.at[pl.ds(at, count), :], sems.at[k])
        )
        copies[-1].start()
        at += count
    return copies


def path_solve(level, read, held, place, wide, total):
    diag_at, off_at = DIAG_AT[level] - LEVEL_AT[level][0], OFF_AT[level] - LEVEL_AT[level][0]
    for n in range(SPECIES):

        def write(at, value, n=n):
            wide[n, at : at + 64, :] = jnp.broadcast_to(value, (64, LANES))

        matvec(held, diag_at, 1, 2**level, functools.partial(read, n), write, OWN)
    for d in range(SLOTS):
        where = place[d : d + 1, :]
        hit = one_hot(jnp.right_shift(where, 7), PATH, 0)
        right = one_hot(jnp.bitwise_and(where, 127), LANES, 0).astype(jnp.bfloat16)
        rows = slice(d * BLOCK, (d + 1) * BLOCK)
        left = []
        for n in range(SPECIES):
            solved = jnp.concatenate([wide[n, rows, :]] * (REACH // LANES), axis=1)
            update = jnp.sum(held[rows, off_at : off_at + REACH] * solved, axis=0, keepdims=True)
            coarse = update.astype(jnp.bfloat16).astype(jnp.float32)
            left += [jnp.where(hit, part, 0.0).astype(jnp.bfloat16) for part in (coarse, update - coarse)]
        product = lax.dot_general(
            jnp.concatenate(left, axis=0), right, (((1,), (1,)), ((), ())), preferred_element_type=jnp.float32
        )
        total[...] = product if d == 0 else total[...] + product


def path_update(level, before, total, path, ahead):
    count = 2 ** (level + 1)
    for n in range(SPECIES):
        at = 2 * n * PATH
        path[n * PATH : (n + 1) * PATH, :] = before[n * PATH : (n + 1) * PATH, :] - (
            total[at : at + PATH, :] + total[at + PATH : at + 2 * PATH, :]
        )
        if ahead is not None:
            ahead[n * count : (n + 1) * count, :] = path[n * PATH + count : n * PATH + 2 * count, :]


def path_first(*refs):
    parts = refs[:PARTS]
    here, path, ahead, r0, places, held, named, turned, wide, total, sems = refs[PARTS:]
    leaf, b = here[0], here[1]
    copies = fetch_parts(parts, 0, held, sems)
    path[...] = jnp.zeros((SPECIES * PATH, LANES), jnp.float32)
    lane = lax.broadcasted_iota(jnp.int32, (BLOCK, LANES), 1)
    row = lax.broadcasted_iota(jnp.int32, (BLOCK, LANES), 0)
    stands = []
    for core in (0, 1):
        for ahead_by in (0, 6, 2, 4):
            slot = jnp.bitwise_and(b + ahead_by, 7) ^ core
            stands.append(jnp.where(lane == row + slot * BLOCK, 1.0, 0.0).astype(jnp.bfloat16))
    order = jnp.concatenate(stands, axis=0)
    for copy in copies:
        copy.wait()
    flipped = jnp.transpose(held[:, RHS_AT : RHS_AT + 256])
    total_rows = None
    for _ in range(3):
        piece = flipped.astype(jnp.bfloat16)
        flipped = flipped - piece.astype(jnp.float32)
        rows = jnp.dot(piece, order, preferred_element_type=jnp.float32)
        total_rows = rows if total_rows is None else total_rows + rows
    turned[...] = total_rows
    for n in range(SPECIES):
        r0[n : n + 1, :] = turned[pl.ds(b * SPECIES + n, 1), :]
        for level in range(1, 6):
            at = n * PATH + 2**level + jnp.bitwise_and(leaf, 2**level - 1)
            path[pl.ds(at, 1), :] = turned[pl.ds(level * 32 + b * SPECIES + n, 1), :]
    named[0] = held[:, 0:LANES]
    named[1] = held[:, LANES : 2 * LANES]
    for level in range(4):
        places[level] = chain_position(named, level, SLOTS) + LANES
    path_solve(0, lambda n, c: r0[n : n + 1, :], held, places.at[0], wide, total)
    path_update(0, path, total, path, ahead)


def path_next(level, *refs):
    parts = refs[:PARTS]
    places, summed, before, path, ahead, held, wide, total, sems = refs[PARTS:]
    copies = fetch_parts(parts, level, held, sems)
    count = 2**level
    for copy in copies:
        copy.wait()
    path_solve(
        level, lambda n, c: summed[n * count + c : n * count + c + 1, :], held, places.at[level], wide, total
    )
    path_update(level, before, total, path, ahead)


def path_last(*refs):
    parts, (place, places, r0, r1, r2, summed, before, keep, send, t2, t3, path, *scratch) = refs[:PARTS], refs[PARTS:]
    path_next(3, *parts, places, summed, before, path, None, *scratch)
    x = place[0]
    even = 1.0 - (x & 1).astype(jnp.float32)
    for n in range(SPECIES):
        slot = n ^ x
        slot = slot ^ (slot >> 1)
        value = jnp.zeros((8, LANES), jnp.float32)
        row = lax.broadcasted_iota(jnp.int32, (8, LANES), 0)
        value = jnp.where(row == x, r0[n : n + 1, :], value)
        for k in range(2):
            value = jnp.where(row == 4 + 2 * (x >> 1) + k, r1[2 * n + k : 2 * n + k + 1, :] * even, value)

        @pl.when(slot < 2)
        def _(n=n, slot=slot, value=value):
            keep[slot, 0:48, :] = path[n * PATH + 16 : (n + 1) * PATH, :]
            keep[slot, 48:56, :] = value

        @pl.when(slot >= 2)
        def _(n=n, slot=slot, value=value):
            send[slot - 2, 0:48, :] = path[n * PATH + 16 : (n + 1) * PATH, :]
            send[slot - 2, 48:56, :] = value

    t2[...] = r2[pl.ds(x * 4, 4), :]
    t3[...] = summed[pl.ds(pl.multiple_of(x * 8, 8), 8), :]


def high_cuts(level):
    columns = COUNT[level] * LANES
    return [
        (DIAG_AT[level], DIAG_AT[level] + columns, 0),
        (OFF_AT[level], OFF_AT[level] + REACH, columns),
    ]


def forward_high(pack, summed, before, solved, residual, held, wide, named, places, sems):
    level, columns = 4, COUNT[4] * LANES
    named_copies = fetch_named(pack, named, sems, 6, 1)
    copies = fetch(pack, held, sems, high_cuts(level))

    def write(at, value):
        wide[at : at + 64, :] = jnp.broadcast_to(value, (64, LANES))
        solved[at : at + 64, 0:1] = value

    copies[0].wait()
    matvec(held, 0, 1, COUNT[level], lambda c: summed[c : c + 1, :], write)
    for copy in named_copies + copies[1:]:
        copy.wait()
    find_places(named, level, places)
    residual[...] = before[...] - scatter_update(held, columns, wide, places, FIRST[5], COUNT[5])


def top(pack, summed, partial, held, wide, sems):
    copies = []
    for k in range(4):
        rows = pl.ds(k * 128, 128)
        copies.append(
            pltpu.make_async_copy(
                pack.at[rows, DIAG_AT[5] : DIAG_AT[5] + 32 * LANES], held.at[rows, :], sems.at[k]
            )
        )
        copies[-1].start()
    for k in range(4):
        copies[k].wait()
        rows = slice(k * 128, (k + 1) * 128)

        def write(at, value, k=k):
            wide[k * 128 + at : k * 128 + at + 64, :] = jnp.broadcast_to(value, (64, LANES))

        matvec(held.at[rows, :], 0, 1, COUNT[5], lambda c: summed[c : c + 1, :], write, 128)

        def write_row(c, value, k=k):
            partial[c : c + 1, :] = value if k == 0 else partial[c : c + 1, :] + value

        matvec_transposed(held.at[rows, :], 0, 1, COUNT[5], wide.at[rows, :], write_row, 128)


def backward_high(level, pack, residual, *rest):
    above = rest[: 5 - level]
    partial, held, wide, chain, named, places, solved, sems = rest[5 - level :]
    columns = COUNT[level] * LANES
    named_copies = fetch_named(pack, named, sems, 6, level - 3)
    copies = fetch(pack, held, sems, high_cuts(level)[::-1])
    for k, value in enumerate(above):
        chain[FIRST[5 - k] : FIRST[5 - k] + COUNT[5 - k], :] = value[...]
    for copy in named_copies:
        copy.wait()
    find_places(named, level, places)
    if level == 4:
        solved = residual
    else:

        def write(at, value):
            solved[at : at + 64, 0:1] = value

        copies[1].wait()
        matvec(held, 0, 1, COUNT[level], lambda c: residual[c : c + 1, :], write)
    copies[0].wait()
    couple(held, columns, chain, places, FIRST[level + 1], solved, 0, wide)
    if level == 4:
        copies[1].wait()

    def write_row(c, value):
        partial[c : c + 1, :] = value

    matvec_transposed(held, 0, 1, COUNT[level], wide, write_row)


def backward_low(pack, r01, r2, s5, s4, s3, out, held, wide, chain, named, places, solved, sems):
    named_copies = fetch_named(pack, named, sems, 6, 0)
    cuts = []
    for level in (2, 1, 0):
        diag_at, off_at = DIAG_AT[level], OFF_AT[level]
        cuts.append((diag_at, diag_at + LANES * 2**level, LANES * (2**level - 1)))
        cuts.append((off_at, off_at + REACH, 896 + REACH * level))
    copies = fetch(pack, held, sems, cuts)
    for level, value in ((5, s5), (4, s4), (3, s3)):
        chain[FIRST[level] : FIRST[level] + COUNT[level], :] = value[...]
    chain[0:16, :] = jnp.zeros((16, LANES), jnp.float32)
    for copy in named_copies:
        copy.wait()
    for k, level in enumerate((2, 1, 0)):
        find_places(named, level, places)

        def write(at, value):
            solved[at : at + 64, 0:1] = value

        def read(c, level=level):
            return r2[c : c + 1, :] if level == 2 else r01[4 * level + c : 4 * level + c + 1, :]

        copies[2 * k].wait()
        matvec(held, LANES * (2**level - 1), 4 >> level, 1 << level, read, write)
        copies[2 * k + 1].wait()
        couple(held, 896 + REACH * level, chain, places, 8, solved, 0, wide)

        def write_row(c, value, first=FIRST[level]):
            chain[first + c : first + c + 1, :] = value

        matvec_transposed(held, LANES * (2**level - 1), 4 >> level, 1 << level, wide, write_row)
    out[...] = chain[0:16, :]


def call(body, outs, scratch, args, far=1, scalar=(), sems=8):
    vmem = pl.BlockSpec(memory_space=pltpu.VMEM)
    smem = pl.BlockSpec(memory_space=pltpu.SMEM)
    hbm = pl.BlockSpec(memory_space=pltpu.HBM)
    specs = [hbm if k < far else smem if k in scalar else vmem for k in range(len(args))]
    return pl.pallas_call(
        body,
        out_shape=outs,
        in_specs=specs,
        out_specs=jax.tree.map(lambda _: vmem, outs),
        scratch_shapes=scratch + [pltpu.SemaphoreType.DMA((sems,))],
        compiler_params=pltpu.CompilerParams(vmem_limit_bytes=(52 if far == 1 else 6) * MIB),
    )(*args)


def shape(*dims, kind=jnp.float32):
    return jax.ShapeDtypeStruct(dims, kind)


def moved(value, axis, to):
    size = lax.axis_size(axis)
    return lax.ppermute(value, axis, [(i, to(i)) for i in range(size)])


def near_x(i):
    return 3 - i


def far_z(i):
    return (i + 5) % 8 if i % 2 else (i + 3) % 8


def sum_leaf(value, first, last):
    steps = [("x", lambda i: i ^ 1), ("x", near_x), ("z", lambda i: i ^ 1)]
    if last < 5:
        steps.append(("z", lambda i: i ^ 2))
    else:
        steps.append(("z", lambda i: (i + 1) % 8 if i % 2 else (i + 7) % 8))
        steps.append(("z", far_z))
    for axis, to in steps[first:last]:
        value = value + moved(value, axis, to)
    return value


def local(rhs, diag_inverse, off_diagonal, rows_index):
    f32 = jnp.float32
    x, z = lax.axis_index("x"), lax.axis_index("z")
    leaf = z * 4 + x
    hbm, vmem = pl.BlockSpec(memory_space=pltpu.HBM), pl.BlockSpec(memory_space=pltpu.VMEM)
    high, low, first, second = pl.pallas_call(
        pack_kernel,
        out_shape=(shape(BLOCK, HIGH), shape(BLOCK, LOW), shape(BLOCK, CUT), shape(BLOCK, LOW - CUT)),
        in_specs=[vmem, vmem, hbm, hbm],
        out_specs=(vmem,) * 4,
        scratch_shapes=[pltpu.SemaphoreType.DMA((18,))],
        compiler_params=pltpu.CompilerParams(vmem_limit_bytes=6 * MIB),
    )(rhs, rows_index, diag_inverse, off_diagonal)
    high = lax.all_gather(high, PLANE, axis=0, tiled=True)
    low = lax.all_gather(low, PLANE, axis=0, tiled=True)

    def group_rows(own):
        down = moved(own, "blk", lambda i: (i + 2) % SLOTS)
        up = moved(own, "blk", lambda i: (i + 6) % SLOTS)
        half = BLOCK // 2
        across = [
            moved(down[:half], "blk", lambda i: (i + 2) % SLOTS),
            moved(up[half:], "blk", lambda i: (i + 6) % SLOTS),
        ]
        here = (own, down, up, *across)
        return here + tuple(moved(part, "blk", lambda i: i ^ 1) for part in here)

    first = group_rows(first)
    second = group_rows(lax.optimization_barrier((second, first[-1]))[0])

    def path_scratch(level, *more):
        return [
            pltpu.VMEM((OWN, LEVEL_AT[level][1] - LEVEL_AT[level][0]), f32),
            *more,
            pltpu.VMEM((SPECIES, OWN, LANES), f32),
            pltpu.VMEM((SPECIES * 2 * PATH, LANES), f32),
        ]

    here = jnp.stack([leaf, lax.axis_index("blk")]).astype(jnp.int32)
    path, ahead, r0, places = call(
        path_first,
        (
            shape(SPECIES * PATH, LANES), shape(SPECIES * 2, LANES), shape(SPECIES, LANES),
            shape(4, SLOTS, REACH, kind=jnp.int32),
        ),
        path_scratch(0, pltpu.VMEM((2, OWN, LANES), f32), pltpu.VMEM((256, LANES), f32)),
        (*first, here),
        far=PARTS,
        scalar=(PARTS,),
        sems=PARTS,
    )
    waiting = [r0, sum_leaf(ahead, 0, 1)]
    for level in (1, 2):
        path, ahead = call(
            functools.partial(path_next, level),
            (shape(SPECIES * PATH, LANES), shape(SPECIES * 2 ** (level + 1), LANES)),
            path_scratch(level),
            (*(first if level < 2 else second), places, waiting[level], path),
            far=PARTS,
            sems=PARTS,
        )
        waiting.append(sum_leaf(ahead, 0, level + 1))
    keep, send, r2, r3 = call(
        path_last,
        (shape(2, 56, LANES), shape(2, 56, LANES), shape(4, LANES), shape(8, LANES)),
        [pltpu.VMEM((SPECIES * PATH, LANES), f32)] + path_scratch(3),
        (*second, x.astype(jnp.int32).reshape(1), places, *waiting, path),
        far=PARTS,
        scalar=(PARTS,),
        sems=PARTS,
    )
    keep = keep + moved(send, "x", near_x)
    turned = keep[0] + moved(keep[1], "x", lambda i: i ^ 1)
    r4 = sum_leaf(turned[0:16], 2, 4)

    wide, chain = pltpu.VMEM((ROWS, LANES), f32), pltpu.VMEM((SPACE, LANES), f32)
    named, places = pltpu.VMEM((2, ROWS, LANES), f32), pltpu.VMEM((BLOCKS, REACH), jnp.int32)
    solved = pltpu.VMEM((ROWS, 8), f32)
    y4, r5 = call(
        forward_high,
        (shape(ROWS, 8), shape(32, LANES)),
        [pltpu.VMEM((ROWS, 16 * LANES + REACH), f32), wide, named, places],
        (high, r4, turned[16:48]),
    )
    r5 = sum_leaf(r5, 2, 5)
    partial = call(top, shape(32, LANES), [pltpu.VMEM((ROWS, 32 * LANES), f32), wide], (high, r5))
    known = [sum_leaf(partial, 2, 5)]
    for level, from_rows in ((4, y4), (3, r3)):
        count = COUNT[level]
        partial = call(
            functools.partial(backward_high, level),
            shape(count, LANES),
            [pltpu.VMEM((ROWS, count * LANES + REACH), f32), wide, chain, named, places, solved],
            (high if level == 4 else low, from_rows, *known),
        )
        known.append(sum_leaf(partial, 2, level))
    last = call(
        backward_low,
        shape(16, LANES),
        [pltpu.VMEM((ROWS, 896 + 3 * REACH), f32), wide, chain, named, places, solved],
        (low, turned[48:56], r2, *known),
    )
    pieces = [last[0:4], last[8:12], last[12:16]]
    for level in (3, 4, 5):
        place = jnp.remainder(z, 2 ** (level - 2)) * 4
        pieces.append(lax.dynamic_slice_in_dim(known[5 - level], place, 4, 0))
    out = jnp.stack(pieces).reshape(6, BLOCKS, BLOCK)
    out = lax.all_to_all(jnp.transpose(out, (1, 0, 2)), PLANE, 0, 0)
    return jnp.transpose(out.reshape(SPECIES, SLOTS, 6, BLOCK), (2, 1, 0, 3)).reshape(6, BLOCKS, BLOCK)


def solution(mesh):
    cut = Mesh(mesh.devices.reshape(8, 4, 8), ("z", "x", "blk"))
    rows = ("z", "x", "blk")
    placed = (P(None, None, rows), P(rows, None), P(None, rows, None), P(None, rows, None))
    return jax.shard_map(
        local, mesh=cut, in_specs=placed, out_specs=P(None, None, rows), check_vma=False
    )
```

time: 1110 us -> 197 us (0.18); the launches traced: 1100 us -> 196 us
  waiting for transfers between devices: 808 us -> 67.3 us
  blocking collectives: 99.3 us -> 14.1 us
  other arithmetic: 49.3 us -> 0.15 us
  local copies, waits for them, and re-layouts: 48.8 us -> 4.92 us
  Pallas kernels: 0 us -> 43.5 us
  starting transfers between devices: 67.2 us -> 52.6 us
    psum x8 -> x0, waiting for transfers between devices: 591 us -> none  [group_total(): summed = lax.psum(partial_value, 'blk')]
    ppermute x30 -> x37, waiting for transfers between devices: 217 us -> 45.2 us  [moved(): return lax.ppermute(value, axis, [(i, to(i)) for i in range(size)])]
    psum x4 -> x0, blocking collectives: 99.3 us -> none  [group_total(): summed = lax.psum(partial_value, 'blk')]
    pallas_call x0 -> x10, Pallas kernels: none -> 43.5 us  [the longest x9 41.9 us: call(): pl.pallas_call(body, out_shape=outs, in_specs=specs, out_specs=jax.tree.m...]
    scatter-add x5 -> x0, other arithmetic: 35.3 us -> none  [local(): pending = pending.at[:, targets].add(-update)]
    all_gather x0 -> x2, waiting for transfers between devices: none -> 21.4 us  [the longest x1 18 us: local(): low = lax.all_gather(low, PLANE, axis=0, tiled=True)]
    gather x5 -> x0, local copies, waits for them, and re-layouts: 16 us -> none  [local(): known = jnp.take(known_chain, targets, axis=1)]
    ppermute x30 -> x37, starting transfers between devices: 66.8 us -> 52.6 us  [moved(): return lax.ppermute(value, axis, [(i, to(i)) for i in range(size)])]
  transfers between devices with their start and end apart: 38 -> 39, of which waited for: 38 -> 27; matrix products, arithmetic and copies ran while one was open for 0% -> 0% of each run, Pallas kernels for 0% -> 12%
where the time goes in v2:
time: 197 us; the launch traced here: 196 us
  waiting for transfers between devices  67.3 us (34%)
  starting transfers between devices  52.6 us (27%)
  Pallas kernels  43.5 us (22%)
  blocking collectives  14.1 us (7%)
  between operations  13.7 us (7%)
  local copies, waits for them, and re-layouts  4.92 us (2%)
    ppermute x37, starting transfers between devices, moved(): return lax.ppermute(value, axis, [(i, to(i)) for i in range(size)])  52.6 us
    ppermute x37, waiting for transfers between devices, moved(): return lax.ppermute(value, axis, [(i, to(i)) for i in range(size)])  45.2 us
    pallas_call x9, Pallas kernels, call(): pl.pallas_call(body, out_shape=outs, in_specs=specs, out_specs=jax.tree.m...  41.9 us
    all_gather x1, waiting for transfers between devices, local(): low = lax.all_gather(low, PLANE, axis=0, tiled=True)  18 us
    all_to_all x1, blocking collectives, local(): out = lax.all_to_all(jnp.transpose(out, (1, 0, 2)), PLANE, 0, 0)  14.1 us
  transfers between devices with their start and end apart: 39, of which 27 were waited for; matrix products, arithmetic and copies ran while one was open for 0% of the time, Pallas kernels for 12%

profile of v2, /device:TPU:1, one launch (start us, length us, event | category | flops | bytes accessed | tf_op | source)
XLA Modules:
  0.0 196.2 jit_solution(144674612777547830)
XLA Ops:
  10.1 1.6 shard_map.46
  12.4 3.6 %collective-permute-start = (f32[16,1920]{1,0:T(8,128)S(1)}, f32[16,1920]{1,0:T(8,128)S(1)}, u32[]{:S(2)}, u32[]{:S(2)}) collective-permute-start(f32[16,1920]{1,0:T(8,128)S(1)} %get-tuple-element.26.refs_0_), channel_id=1, source_target_pairs={{0,6},{1,7},{2,0},{3,1},{4,2},{5,3},{6,4},{7,5},{8,14},{9,15},{10,... | collective-permute-start | bytes 368648 | tf_op jit(solution)/shard_map/ppermute | solution.py:441
  16.1 1.9 collective-permute-done.refs_2_
  18.0 3.5 %collective-permute-start.1 = (f32[8,1920]{1,0:T(8,128)S(1)}, f32[8,1920]{1,0:T(8,128)S(1)}, u32[]{:S(2)}, u32[]{:S(2)}) collective-permute-start(f32[8,1920]{1,0:T(8,128)S(1)} %slice.48), channel_id=1, source_target_pairs={{0,6},{1,7},{2,0},{3,1},{4,2},{5,3},{6,4},{7,5},{8,14},{9,15},{10,... | collective-permute-start | bytes 184328 | tf_op jit(solution)/shard_map/ppermute | solution.py:441
  21.5 1.8 collective-permute-start.14
  23.3 1.9 collective-permute-start.2
  26.5 2.9 %collective-permute-start.4 = (f32[16,2560]{1,0:T(8,128)S(1)}, f32[16,2560]{1,0:T(8,128)S(1)}, u32[]{:S(2)}, u32[]{:S(2)}) collective-permute-start(f32[16,2560]{1,0:T(8,128)S(1)} %get-tuple-element.27.refs_0_), channel_id=1, source_target_pairs={{0,6},{1,7},{2,0},{3,1},{4,2},{5,3},{6,4},{7,5},{8,14},{9,15},{10,... | collective-permute-start | bytes 491528 | tf_op jit(solution)/shard_map/ppermute | solution.py:441
  32.6 2.8 %shard_map.47 = (f32[256,128]{1,0:T(8,128)S(1)}, f32[8,128]{1,0:T(8,128)S(1)}, f32[4,128]{1,0:T(4,128)S(1)}, s32[4,8,512]{2,1,0:T(8,128)S(1)}) custom-call(f32[16,1920]{1,0:T(8,128)S(1)} %get-tuple-element.26.refs_0_, f32[16,1920]{1,0:T(8,128)S(1)} %collective-permute-done.12.refs_1_, f32[16,1920]{1,0:T(8,128)S(1)} %collective-permute-done.refs_2_, ...), custom_call_target="tpu_custom_call" | custom-call | tf_op jit(solution)/shard_map/pallas_call | solution.py:425
  36.7 1.7 collective-permute-done.18
  38.4 1.7 shard_map.48
  41.4 1.7 collective-permute-done.19
  43.1 2.5 %collective-permute-start.20 = (f32[16,128]{1,0:T(8,128)S(1)}, f32[16,128]{1,0:T(8,128)S(1)}, u32[]{:S(2)}, u32[]{:S(2)}) collective-permute-start(f32[16,128]{1,0:T(8,128)S(1)} %add.81), channel_id=1, source_target_pairs={{0,24},{8,16},{16,8},{24,0},{1,25},{9,17},{17,9},{25,1},{2,26},{10... | collective-permute-start | bytes 24584 | tf_op jit(solution)/shard_map/ppermute | solution.py:441
  45.6 2.1 %collective-permute-start.7 = (f32[16,2560]{1,0:T(8,128)S(1)}, f32[16,2560]{1,0:T(8,128)S(1)}, u32[]{:S(2)}, u32[]{:S(2)}) collective-permute-start(f32[16,2560]{1,0:T(8,128)S(1)} %get-tuple-element.27.refs_0_), channel_id=1, source_target_pairs={{0,1},{1,0},{2,3},{3,2},{4,5},{5,4},{6,7},{7,6},{8,9},{9,8},{10,11... | collective-permute-start | bytes 491528 | tf_op jit(solution)/shard_map/ppermute | solution.py:441
  47.8 2.7 %collective-permute-start.6 = (f32[8,2560]{1,0:T(8,128)S(1)}, f32[8,2560]{1,0:T(8,128)S(1)}, u32[]{:S(2)}, u32[]{:S(2)}) collective-permute-start(f32[8,2560]{1,0:T(8,128)S(1)} %slice.50), channel_id=1, source_target_pairs={{0,6},{1,7},{2,0},{3,1},{4,2},{5,3},{6,4},{7,5},{8,14},{9,15},{10,... | collective-permute-start | bytes 245768 | tf_op jit(solution)/shard_map/ppermute | solution.py:441
  51.1 1.9 collective-permute-done.5.refs_3_
  55.2 1.8 shard_map.49
  57.1 3.3 %collective-permute-done.21 = f32[32,128]{1,0:T(8,128)S(1)} collective-permute-done((f32[32,128]{1,0:T(8,128)S(1)}, f32[32,128]{1,0:T(8,128)S(1)}, u32[]{:S(2)}, u32[]{:S(2)}) %collective-permute-start.21) | collective-permute-done | bytes 16416 | tf_op jit(solution)/shard_map/ppermute | solution.py:441
  60.4 4.5 %collective-permute-done.22 = f32[32,128]{1,0:T(8,128)S(1)} collective-permute-done((f32[32,128]{1,0:T(8,128)S(1)}, f32[32,128]{1,0:T(8,128)S(1)}, u32[]{:S(2)}, u32[]{:S(2)}) %collective-permute-start.22) | collective-permute-done | bytes 16416 | tf_op jit(solution)/shard_map/ppermute | solution.py:441
  64.9 1.6 collective-permute-start.23
  66.6 1.5 collective-permute-done.23
  68.1 2.2 %shard_map.50 = (f32[2,56,128]{2,1,0:T(8,128)S(1)}, f32[2,56,128]{2,1,0:T(8,128)S(1)}, f32[4,128]{1,0:T(4,128)S(1)}, f32[8,128]{1,0:T(8,128)S(1)}) custom-call(f32[16,2560]{1,0:T(8,128)S(1)} %get-tuple-element.27.refs_0_, f32[16,2560]{1,0:T(8,128)S(1)} %collective-permute-done.3.refs_1_, f32[16,2560]{1,0:T(8,128)S(1)} %collective-permute-done.4.refs_2_, ...), custom_call_target="tpu_custom_call" | custom-call | tf_op jit(solution)/shard_map/pallas_call | solution.py:425
  70.4 5.8 %collective-permute-done.24 = f32[2,56,128]{2,1,0:T(8,128)S(1)} collective-permute-done((f32[2,56,128]{2,1,0:T(8,128)S(1)}, f32[2,56,128]{2,1,0:T(8,128)S(1)}, u32[]{:S(2)}, u32[]{:S(2)}) %collective-permute-start.24) | collective-permute-done | bytes 57376 | tf_op jit(solution)/shard_map/ppermute | solution.py:441
  76.3 3.7 %collective-permute-done.25 = f32[56,128]{1,0:T(8,128)S(1)} collective-permute-done((f32[56,128]{1,0:T(8,128)S(1)}, f32[56,128]{1,0:T(8,128)S(1)}, u32[]{:S(2)}, u32[]{:S(2)}) %collective-permute-start.25) | collective-permute-done | bytes 28704 | tf_op jit(solution)/shard_map/ppermute | solution.py:441
  80.1 1.5 collective-permute-start.26
  81.6 1.4 collective-permute-done.26
  83.0 3.0 %collective-permute-start.27 = (f32[16,128]{1,0:T(8,128)S(1)}, f32[16,128]{1,0:T(8,128)S(1)}, u32[]{:S(2)}, u32[]{:S(2)}) collective-permute-start(f32[16,128]{1,0:T(8,128)S(1)} %slice_add_fusion), channel_id=1, source_target_pairs={{0,64},{32,96},{64,0},{96,32},{128,192},{160,224},{192,128},{224,1... | collective-permute-start | bytes 24584 | tf_op jit(solution)/shard_map/ppermute | solution.py:441
  86.0 1.4 collective-permute-done.27
  87.5 3.4 %all-gather.5.cloned.1.call-done.pack = f32[512,6912]{1,0:T(8,128)} async-done(((f32[16,6912]{1,0:T(8,128)}), f32[512,6912]{1,0:T(8,128)}) %all-gather.5.cloned.1.call-update) | async-done | bytes 14155792 | tf_op jit(solution)/shard_map/all_gather | solution.py:477
  90.9 5.3 %shard_map.51 = (f32[512,8]{1,0:T(8,128)S(1)}, f32[32,128]{1,0:T(8,128)S(1)}) custom-call(f32[512,6912]{1,0:T(8,128)} %all-gather.5.cloned.1.call-done.pack, f32[16,128]{1,0:T(8,128)S(1)} %add.89.summed, f32[32,128]{1,0:T(8,128)S(1)} %slice.56.before), custom_call_target="tpu_custom_call" | custom-call | tf_op jit(solution)/shard_map/pallas_call | solution.py:425
  96.2 1.4 collective-permute-start.28
  98.8 3.0 %collective-permute-start.29 = (f32[32,128]{1,0:T(8,128)S(1)}, f32[32,128]{1,0:T(8,128)S(1)}, u32[]{:S(2)}, u32[]{:S(2)}) collective-permute-start(f32[32,128]{1,0:T(8,128)S(1)} %add.90), channel_id=1, source_target_pairs={{0,224},{32,64},{64,32},{96,128},{128,96},{160,192},{192,160},{224... | collective-permute-start | bytes 49160 | tf_op jit(solution)/shard_map/ppermute | solution.py:441
  103.0 2.9 %collective-permute-start.30 = (f32[32,128]{1,0:T(8,128)S(1)}, f32[32,128]{1,0:T(8,128)S(1)}, u32[]{:S(2)}, u32[]{:S(2)}) collective-permute-start(f32[32,128]{1,0:T(8,128)S(1)} %add.91), channel_id=1, source_target_pairs={{0,96},{32,192},{64,160},{96,0},{128,224},{160,64},{192,32},{224,1... | collective-permute-start | bytes 49160 | tf_op jit(solution)/shard_map/ppermute | solution.py:441
  105.9 1.5 collective-permute-done.30
  107.4 3.9 %shard_map.52 = f32[32,128]{1,0:T(8,128)S(1)} custom-call(f32[512,6912]{1,0:T(8,128)} %all-gather.5.cloned.1.call-done.pack, f32[32,128]{1,0:T(8,128)S(1)} %add.92.summed), custom_call_target="tpu_custom_call" | custom-call | tf_op jit(solution)/shard_map/pallas_call | solution.py:425
  112.5 1.9 collective-permute-done.31
  114.4 2.7 %collective-permute-start.32 = (f32[32,128]{1,0:T(8,128)S(1)}, f32[32,128]{1,0:T(8,128)S(1)}, u32[]{:S(2)}, u32[]{:S(2)}) collective-permute-start(f32[32,128]{1,0:T(8,128)S(1)} %add.93), channel_id=1, source_target_pairs={{0,224},{32,64},{64,32},{96,128},{128,96},{160,192},{192,160},{224... | collective-permute-start | bytes 49160 | tf_op jit(solution)/shard_map/ppermute | solution.py:441
  117.1 1.5 collective-permute-done.32
  118.6 3.0 %collective-permute-start.33 = (f32[32,128]{1,0:T(8,128)S(1)}, f32[32,128]{1,0:T(8,128)S(1)}, u32[]{:S(2)}, u32[]{:S(2)}) collective-permute-start(f32[32,128]{1,0:T(8,128)S(1)} %add.94), channel_id=1, source_target_pairs={{0,96},{32,192},{64,160},{96,0},{128,224},{160,64},{192,32},{224,1... | collective-permute-start | bytes 49160 | tf_op jit(solution)/shard_map/ppermute | solution.py:441
  121.6 1.4 collective-permute-done.33
  123.0 5.1 %shard_map.53 = f32[16,128]{1,0:T(8,128)S(1)} custom-call(f32[512,6912]{1,0:T(8,128)} %all-gather.5.cloned.1.call-done.pack, f32[512,8]{1,0:T(8,128)S(1)} %get-tuple-element.41.residual, f32[32,128]{1,0:T(8,128)S(1)} %add.95.rest_0_.s5), custom_call_target="tpu_custom_call" | custom-call | tf_op jit(solution)/shard_map/pallas_call | solution.py:425
  129.3 1.4 collective-permute-done.34
  130.7 2.3 %collective-permute-start.35 = (f32[16,128]{1,0:T(8,128)S(1)}, f32[16,128]{1,0:T(8,128)S(1)}, u32[]{:S(2)}, u32[]{:S(2)}) collective-permute-start(f32[16,128]{1,0:T(8,128)S(1)} %add.96), channel_id=1, source_target_pairs={{0,64},{32,96},{64,0},{96,32},{128,192},{160,224},{192,128},{224,1... | collective-permute-start | bytes 24584 | tf_op jit(solution)/shard_map/ppermute | solution.py:441
  133.1 1.4 collective-permute-done.35
  134.5 18.0 %all-gather.3.cloned.1.call-done.pack = f32[512,4480]{1,0:T(8,128)} async-done(((f32[16,4480]{1,0:T(8,128)}), f32[512,4480]{1,0:T(8,128)}) %all-gather.3.cloned.1.call-update) | async-done | bytes 9175056 | tf_op jit(solution)/shard_map/all_gather | solution.py:478
  152.4 6.0 %shard_map.54 = f32[8,128]{1,0:T(8,128)S(1)} custom-call(f32[512,4480]{1,0:T(8,128)} %all-gather.3.cloned.1.call-done.pack, f32[8,128]{1,0:T(8,128)S(1)} %get-tuple-element.42.residual, f32[32,128]{1,0:T(8,128)S(1)} %add.95.rest_0_.s5, f32[16,128]{1,0:T(8,128)S(1)} %add.97.rest_1_.s4), custom_call_target="tpu_custom_call" | custom-call | tf_op jit(solution)/shard_map/pallas_call | solution.py:425
  158.5 1.4 collective-permute-start.36
  161.0 13.0 %shard_map.55 = f32[16,128]{1,0:T(8,128)S(1)} custom-call(f32[512,4480]{1,0:T(8,128)} %all-gather.3.cloned.1.call-done.pack, f32[8,128]{1,0:T(8,128)S(1)} %slice.54.r01, f32[4,128]{1,0:T(4,128)S(1)} %get-tuple-element.38.r2, f32[32,128]{1,0:T(8,128)S(1)} %add.95.rest_0_.s5, f32[16,128]{1,0:T(8,128)S(1)} %add.97.rest_1_.s4, f32[8,128]{1,0:T(8,128)S(1)} %add.98.s3), custom_call_target="tpu_custom_call" | custom-call | tf_op jit(solution)/shard_map/pallas_call | solution.py:425
  174.5 14.1 %all_to_all.5 = f32[32,6,16]{2,1,0:T(8,128)S(1)} all-to-all(f32[32,6,16]{2,1,0:T(8,128)S(1)} %copy.11), channel_id=1, replica_groups=mesh['z'=8,'x'=4,'blk'=8] {'x','blk'}, dimensions={0} | all-to-all | bytes 24576 | tf_op jit(solution)/shard_map/all_to_all | solution.py:571
  (97 shorter events, 21.8 us)
Async XLA Ops:
  6.5 84.3 %all-gather.5.cloned.1.call-start = ((), (), s32[]{:S(2)}) async-start(), calls=%async_computation.2 | async-start | bytes 14598144 | tf_op jit(solution)/shard_map/all_gather | solution.py:477
  7.4 1.0 copy-start
  8.5 0.9 copy-start.1
  9.4 0.7 copy-start.2
  11.7 140.8 %all-gather.3.cloned.1.call-start = ((), (), s32[]{:S(2)}) async-start(), calls=%async_computation.1 | async-start | bytes 9461760 | tf_op jit(solution)/shard_map/all_gather | solution.py:478
  12.4 5.5 %collective-permute-start = (f32[16,1920]{1,0:T(8,128)S(1)}, f32[16,1920]{1,0:T(8,128)S(1)}, u32[]{:S(2)}, u32[]{:S(2)}) collective-permute-start(f32[16,1920]{1,0:T(8,128)S(1)} %get-tuple-element.26.refs_0_), channel_id=1, source_target_pairs={{0,6},{1,7},{2,0},{3,1},{4,2},{5,3},{6,4},{7,5},{8,14},{9,15},{10,... | collective-permute-start | bytes 368648 | tf_op jit(solution)/shard_map/ppermute | solution.py:441
  16.1 9.1 %collective-permute-start.12 = (f32[16,1920]{1,0:T(8,128)S(1)}, f32[16,1920]{1,0:T(8,128)S(1)}, u32[]{:S(2)}, u32[]{:S(2)}) collective-permute-start(f32[16,1920]{1,0:T(8,128)S(1)} %get-tuple-element.26.refs_0_), channel_id=1, source_target_pairs={{0,2},{1,3},{2,4},{3,5},{4,6},{5,7},{6,0},{7,1},{8,10},{9,11},{10,... | collective-permute-start | bytes 368648 | tf_op jit(solution)/shard_map/ppermute | solution.py:441
  18.0 5.4 %collective-permute-start.1 = (f32[8,1920]{1,0:T(8,128)S(1)}, f32[8,1920]{1,0:T(8,128)S(1)}, u32[]{:S(2)}, u32[]{:S(2)}) collective-permute-start(f32[8,1920]{1,0:T(8,128)S(1)} %slice.48), channel_id=1, source_target_pairs={{0,6},{1,7},{2,0},{3,1},{4,2},{5,3},{6,4},{7,5},{8,14},{9,15},{10,... | collective-permute-start | bytes 184328 | tf_op jit(solution)/shard_map/ppermute | solution.py:441
  21.5 8.5 %collective-permute-start.14 = (f32[16,1920]{1,0:T(8,128)S(1)}, f32[16,1920]{1,0:T(8,128)S(1)}, u32[]{:S(2)}, u32[]{:S(2)}) collective-permute-start(f32[16,1920]{1,0:T(8,128)S(1)} %get-tuple-element.26.refs_0_), channel_id=1, source_target_pairs={{0,1},{1,0},{2,3},{3,2},{4,5},{5,4},{6,7},{7,6},{8,9},{9,8},{10,11... | collective-permute-start | bytes 368648 | tf_op jit(solution)/shard_map/ppermute | solution.py:441
  23.3 2.8 %collective-permute-start.2 = (f32[8,1920]{1,0:T(8,128)S(1)}, f32[8,1920]{1,0:T(8,128)S(1)}, u32[]{:S(2)}, u32[]{:S(2)}) collective-permute-start(f32[8,1920]{1,0:T(8,128)S(1)} %collective-permute-done.1.refs_4_), channel_id=1, source_target_pairs={{0,1},{1,0},{2,3},{3,2},{4,5},{5,4},{6,7},{7,6},{8,9},{9,8},{10,11... | collective-permute-start | bytes 184328 | tf_op jit(solution)/shard_map/ppermute | solution.py:441
  25.2 5.7 %collective-permute-start.13 = (f32[8,1920]{1,0:T(8,128)S(1)}, f32[8,1920]{1,0:T(8,128)S(1)}, u32[]{:S(2)}, u32[]{:S(2)}) collective-permute-start(f32[8,1920]{1,0:T(8,128)S(1)} %slice.51), channel_id=1, source_target_pairs={{0,2},{1,3},{2,4},{3,5},{4,6},{5,7},{6,0},{7,1},{8,10},{9,11},{10,... | collective-permute-start | bytes 184328 | tf_op jit(solution)/shard_map/ppermute | solution.py:441
  26.1 21.6 %collective-permute-start.3 = (f32[16,2560]{1,0:T(8,128)S(1)}, f32[16,2560]{1,0:T(8,128)S(1)}, u32[]{:S(2)}, u32[]{:S(2)}) collective-permute-start(f32[16,2560]{1,0:T(8,128)S(1)} %get-tuple-element.27.refs_0_), channel_id=1, source_target_pairs={{0,2},{1,3},{2,4},{3,5},{4,6},{5,7},{6,0},{7,1},{8,10},{9,11},{10,... | collective-permute-start | bytes 491528 | tf_op jit(solution)/shard_map/ppermute | solution.py:441
  26.5 21.4 %collective-permute-start.4 = (f32[16,2560]{1,0:T(8,128)S(1)}, f32[16,2560]{1,0:T(8,128)S(1)}, u32[]{:S(2)}, u32[]{:S(2)}) collective-permute-start(f32[16,2560]{1,0:T(8,128)S(1)} %get-tuple-element.27.refs_0_), channel_id=1, source_target_pairs={{0,6},{1,7},{2,0},{3,1},{4,2},{5,3},{6,4},{7,5},{8,14},{9,15},{10,... | collective-permute-start | bytes 491528 | tf_op jit(solution)/shard_map/ppermute | solution.py:441
  29.4 3.2 %collective-permute-start.15 = (f32[16,1920]{1,0:T(8,128)S(1)}, f32[16,1920]{1,0:T(8,128)S(1)}, u32[]{:S(2)}, u32[]{:S(2)}) collective-permute-start(f32[16,1920]{1,0:T(8,128)S(1)} %collective-permute-done.12.refs_1_), channel_id=1, source_target_pairs={{0,1},{1,0},{2,3},{3,2},{4,5},{5,4},{6,7},{7,6},{8,9},{9,8},{10,11... | collective-permute-start | bytes 368648 | tf_op jit(solution)/shard_map/ppermute | solution.py:441
  30.0 2.6 %collective-permute-start.16 = (f32[16,1920]{1,0:T(8,128)S(1)}, f32[16,1920]{1,0:T(8,128)S(1)}, u32[]{:S(2)}, u32[]{:S(2)}) collective-permute-start(f32[16,1920]{1,0:T(8,128)S(1)} %collective-permute-done.refs_2_), channel_id=1, source_target_pairs={{0,1},{1,0},{2,3},{3,2},{4,5},{5,4},{6,7},{7,6},{8,9},{9,8},{10,11... | collective-permute-start | bytes 368648 | tf_op jit(solution)/shard_map/ppermute | solution.py:441
  30.9 1.7 collective-permute-start.17
  35.4 3.0 %collective-permute-start.18 = (f32[8,128]{1,0:T(8,128)S(1)}, f32[8,128]{1,0:T(8,128)S(1)}, u32[]{:S(2)}, u32[]{:S(2)}) collective-permute-start(f32[8,128]{1,0:T(8,128)S(1)} %get-tuple-element.30), channel_id=1, source_target_pairs={{0,8},{8,0},{16,24},{24,16},{1,9},{9,1},{17,25},{25,17},{2,10},{10... | collective-permute-start | bytes 12296 | tf_op jit(solution)/shard_map/ppermute | solution.py:441
  40.1 3.0 %collective-permute-start.19 = (f32[16,128]{1,0:T(8,128)S(1)}, f32[16,128]{1,0:T(8,128)S(1)}, u32[]{:S(2)}, u32[]{:S(2)}) collective-permute-start(f32[16,128]{1,0:T(8,128)S(1)} %get-tuple-element.32), channel_id=1, source_target_pairs={{0,8},{8,0},{16,24},{24,16},{1,9},{9,1},{17,25},{25,17},{2,10},{10... | collective-permute-start | bytes 24584 | tf_op jit(solution)/shard_map/ppermute | solution.py:441
  43.1 8.0 %collective-permute-start.20 = (f32[16,128]{1,0:T(8,128)S(1)}, f32[16,128]{1,0:T(8,128)S(1)}, u32[]{:S(2)}, u32[]{:S(2)}) collective-permute-start(f32[16,128]{1,0:T(8,128)S(1)} %add.81), channel_id=1, source_target_pairs={{0,24},{8,16},{16,8},{24,0},{1,25},{9,17},{17,9},{25,1},{2,26},{10... | collective-permute-start | bytes 24584 | tf_op jit(solution)/shard_map/ppermute | solution.py:441
  45.6 8.3 %collective-permute-start.7 = (f32[16,2560]{1,0:T(8,128)S(1)}, f32[16,2560]{1,0:T(8,128)S(1)}, u32[]{:S(2)}, u32[]{:S(2)}) collective-permute-start(f32[16,2560]{1,0:T(8,128)S(1)} %get-tuple-element.27.refs_0_), channel_id=1, source_target_pairs={{0,1},{1,0},{2,3},{3,2},{4,5},{5,4},{6,7},{7,6},{8,9},{9,8},{10,11... | collective-permute-start | bytes 491528 | tf_op jit(solution)/shard_map/ppermute | solution.py:441
  47.7 5.4 %collective-permute-start.5 = (f32[8,2560]{1,0:T(8,128)S(1)}, f32[8,2560]{1,0:T(8,128)S(1)}, u32[]{:S(2)}, u32[]{:S(2)}) collective-permute-start(f32[8,2560]{1,0:T(8,128)S(1)} %slice.49), channel_id=1, source_target_pairs={{0,2},{1,3},{2,4},{3,5},{4,6},{5,7},{6,0},{7,1},{8,10},{9,11},{10,... | collective-permute-start | bytes 245768 | tf_op jit(solution)/shard_map/ppermute | solution.py:441
  47.8 6.0 %collective-permute-start.6 = (f32[8,2560]{1,0:T(8,128)S(1)}, f32[8,2560]{1,0:T(8,128)S(1)}, u32[]{:S(2)}, u32[]{:S(2)}) collective-permute-start(f32[8,2560]{1,0:T(8,128)S(1)} %slice.50), channel_id=1, source_target_pairs={{0,6},{1,7},{2,0},{3,1},{4,2},{5,3},{6,4},{7,5},{8,14},{9,15},{10,... | collective-permute-start | bytes 245768 | tf_op jit(solution)/shard_map/ppermute | solution.py:441
  50.6 4.6 %collective-permute-start.8 = (f32[16,2560]{1,0:T(8,128)S(1)}, f32[16,2560]{1,0:T(8,128)S(1)}, u32[]{:S(2)}, u32[]{:S(2)}) collective-permute-start(f32[16,2560]{1,0:T(8,128)S(1)} %collective-permute-done.3.refs_1_), channel_id=1, source_target_pairs={{0,1},{1,0},{2,3},{3,2},{4,5},{5,4},{6,7},{7,6},{8,9},{9,8},{10,11... | collective-permute-start | bytes 491528 | tf_op jit(solution)/shard_map/ppermute | solution.py:441
  51.1 4.0 %collective-permute-start.9 = (f32[16,2560]{1,0:T(8,128)S(1)}, f32[16,2560]{1,0:T(8,128)S(1)}, u32[]{:S(2)}, u32[]{:S(2)}) collective-permute-start(f32[16,2560]{1,0:T(8,128)S(1)} %collective-permute-done.4.refs_2_), channel_id=1, source_target_pairs={{0,1},{1,0},{2,3},{3,2},{4,5},{5,4},{6,7},{7,6},{8,9},{9,8},{10,11... | collective-permute-start | bytes 491528 | tf_op jit(solution)/shard_map/ppermute | solution.py:441
  53.1 1.7 collective-permute-start.10
  53.9 1.3 collective-permute-start.11
  57.0 3.4 %collective-permute-start.21 = (f32[32,128]{1,0:T(8,128)S(1)}, f32[32,128]{1,0:T(8,128)S(1)}, u32[]{:S(2)}, u32[]{:S(2)}) collective-permute-start(f32[32,128]{1,0:T(8,128)S(1)} %get-tuple-element.34), channel_id=1, source_target_pairs={{0,8},{8,0},{16,24},{24,16},{1,9},{9,1},{17,25},{25,17},{2,10},{10... | collective-permute-start | bytes 49160 | tf_op jit(solution)/shard_map/ppermute | solution.py:441
  60.4 4.5 %collective-permute-start.22 = (f32[32,128]{1,0:T(8,128)S(1)}, f32[32,128]{1,0:T(8,128)S(1)}, u32[]{:S(2)}, u32[]{:S(2)}) collective-permute-start(f32[32,128]{1,0:T(8,128)S(1)} %add.83), channel_id=1, source_target_pairs={{0,24},{8,16},{16,8},{24,0},{1,25},{9,17},{17,9},{25,1},{2,26},{10... | collective-permute-start | bytes 49160 | tf_op jit(solution)/shard_map/ppermute | solution.py:441
  64.9 3.2 %collective-permute-start.23 = (f32[32,128]{1,0:T(8,128)S(1)}, f32[32,128]{1,0:T(8,128)S(1)}, u32[]{:S(2)}, u32[]{:S(2)}) collective-permute-start(f32[32,128]{1,0:T(8,128)S(1)} %add.84), channel_id=1, source_target_pairs={{0,32},{32,0},{64,96},{96,64},{128,160},{160,128},{192,224},{224,1... | collective-permute-start | bytes 49160 | tf_op jit(solution)/shard_map/ppermute | solution.py:441
  70.3 5.9 %collective-permute-start.24 = (f32[2,56,128]{2,1,0:T(8,128)S(1)}, f32[2,56,128]{2,1,0:T(8,128)S(1)}, u32[]{:S(2)}, u32[]{:S(2)}) collective-permute-start(f32[2,56,128]{2,1,0:T(8,128)S(1)} %get-tuple-element.37), channel_id=1, source_target_pairs={{0,24},{8,16},{16,8},{24,0},{1,25},{9,17},{17,9},{25,1},{2,26},{10... | collective-permute-start | bytes 172040 | tf_op jit(solution)/shard_map/ppermute | solution.py:441
  76.2 3.8 %collective-permute-start.25 = (f32[56,128]{1,0:T(8,128)S(1)}, f32[56,128]{1,0:T(8,128)S(1)}, u32[]{:S(2)}, u32[]{:S(2)}) collective-permute-start(f32[56,128]{1,0:T(8,128)S(1)} %slice_bitcast_fusion), channel_id=1, source_target_pairs={{0,8},{8,0},{16,24},{24,16},{1,9},{9,1},{17,25},{25,17},{2,10},{10... | collective-permute-start | bytes 86024 | tf_op jit(solution)/shard_map/ppermute | solution.py:441
  80.1 3.0 %collective-permute-start.26 = (f32[16,128]{1,0:T(8,128)S(1)}, f32[16,128]{1,0:T(8,128)S(1)}, u32[]{:S(2)}, u32[]{:S(2)}) collective-permute-start(f32[16,128]{1,0:T(8,128)S(1)} %slice.55), channel_id=1, source_target_pairs={{0,32},{32,0},{64,96},{96,64},{128,160},{160,128},{192,224},{224,1... | collective-permute-start | bytes 24584 | tf_op jit(solution)/shard_map/ppermute | solution.py:441
  83.0 4.4 %collective-permute-start.27 = (f32[16,128]{1,0:T(8,128)S(1)}, f32[16,128]{1,0:T(8,128)S(1)}, u32[]{:S(2)}, u32[]{:S(2)}) collective-permute-start(f32[16,128]{1,0:T(8,128)S(1)} %slice_add_fusion), channel_id=1, source_target_pairs={{0,64},{32,96},{64,0},{96,32},{128,192},{160,224},{192,128},{224,1... | collective-permute-start | bytes 24584 | tf_op jit(solution)/shard_map/ppermute | solution.py:441
  96.2 2.7 %collective-permute-start.28 = (f32[32,128]{1,0:T(8,128)S(1)}, f32[32,128]{1,0:T(8,128)S(1)}, u32[]{:S(2)}, u32[]{:S(2)}) collective-permute-start(f32[32,128]{1,0:T(8,128)S(1)} %get-tuple-element.40), channel_id=1, source_target_pairs={{0,32},{32,0},{64,96},{96,64},{128,160},{160,128},{192,224},{224,1... | collective-permute-start | bytes 49160 | tf_op jit(solution)/shard_map/ppermute | solution.py:441
  98.8 4.2 %collective-permute-start.29 = (f32[32,128]{1,0:T(8,128)S(1)}, f32[32,128]{1,0:T(8,128)S(1)}, u32[]{:S(2)}, u32[]{:S(2)}) collective-permute-start(f32[32,128]{1,0:T(8,128)S(1)} %add.90), channel_id=1, source_target_pairs={{0,224},{32,64},{64,32},{96,128},{128,96},{160,192},{192,160},{224... | collective-permute-start | bytes 49160 | tf_op jit(solution)/shard_map/ppermute | solution.py:441
  103.0 4.4 %collective-permute-start.30 = (f32[32,128]{1,0:T(8,128)S(1)}, f32[32,128]{1,0:T(8,128)S(1)}, u32[]{:S(2)}, u32[]{:S(2)}) collective-permute-start(f32[32,128]{1,0:T(8,128)S(1)} %add.91), channel_id=1, source_target_pairs={{0,96},{32,192},{64,160},{96,0},{128,224},{160,64},{192,32},{224,1... | collective-permute-start | bytes 49160 | tf_op jit(solution)/shard_map/ppermute | solution.py:441
  111.3 3.1 %collective-permute-start.31 = (f32[32,128]{1,0:T(8,128)S(1)}, f32[32,128]{1,0:T(8,128)S(1)}, u32[]{:S(2)}, u32[]{:S(2)}) collective-permute-start(f32[32,128]{1,0:T(8,128)S(1)} %shard_map.52), channel_id=1, source_target_pairs={{0,32},{32,0},{64,96},{96,64},{128,160},{160,128},{192,224},{224,1... | collective-permute-start | bytes 49160 | tf_op jit(solution)/shard_map/ppermute | solution.py:441
  114.4 4.2 %collective-permute-start.32 = (f32[32,128]{1,0:T(8,128)S(1)}, f32[32,128]{1,0:T(8,128)S(1)}, u32[]{:S(2)}, u32[]{:S(2)}) collective-permute-start(f32[32,128]{1,0:T(8,128)S(1)} %add.93), channel_id=1, source_target_pairs={{0,224},{32,64},{64,32},{96,128},{128,96},{160,192},{192,160},{224... | collective-permute-start | bytes 49160 | tf_op jit(solution)/shard_map/ppermute | solution.py:441
  118.6 4.4 %collective-permute-start.33 = (f32[32,128]{1,0:T(8,128)S(1)}, f32[32,128]{1,0:T(8,128)S(1)}, u32[]{:S(2)}, u32[]{:S(2)}) collective-permute-start(f32[32,128]{1,0:T(8,128)S(1)} %add.94), channel_id=1, source_target_pairs={{0,96},{32,192},{64,160},{96,0},{128,224},{160,64},{192,32},{224,1... | collective-permute-start | bytes 49160 | tf_op jit(solution)/shard_map/ppermute | solution.py:441
  128.1 2.6 %collective-permute-start.34 = (f32[16,128]{1,0:T(8,128)S(1)}, f32[16,128]{1,0:T(8,128)S(1)}, u32[]{:S(2)}, u32[]{:S(2)}) collective-permute-start(f32[16,128]{1,0:T(8,128)S(1)} %shard_map.53), channel_id=1, source_target_pairs={{0,32},{32,0},{64,96},{96,64},{128,160},{160,128},{192,224},{224,1... | collective-permute-start | bytes 24584 | tf_op jit(solution)/shard_map/ppermute | solution.py:441
  130.7 3.8 %collective-permute-start.35 = (f32[16,128]{1,0:T(8,128)S(1)}, f32[16,128]{1,0:T(8,128)S(1)}, u32[]{:S(2)}, u32[]{:S(2)}) collective-permute-start(f32[16,128]{1,0:T(8,128)S(1)} %add.96), channel_id=1, source_target_pairs={{0,64},{32,96},{64,0},{96,32},{128,192},{160,224},{192,128},{224,1... | collective-permute-start | bytes 24584 | tf_op jit(solution)/shard_map/ppermute | solution.py:441
  158.5 2.5 %collective-permute-start.36 = (f32[8,128]{1,0:T(8,128)S(1)}, f32[8,128]{1,0:T(8,128)S(1)}, u32[]{:S(2)}, u32[]{:S(2)}) collective-permute-start(f32[8,128]{1,0:T(8,128)S(1)} %shard_map.54), channel_id=1, source_target_pairs={{0,32},{32,0},{64,96},{96,64},{128,160},{160,128},{192,224},{224,1... | collective-permute-start | bytes 12296 | tf_op jit(solution)/shard_map/ppermute | solution.py:441
Sparse Core Ops, SparseCore 0:
  11.8 79.0 all-gather.4
  93.4 58.9 all-gather.2
